TPU v7x, 128 devices: a whole 4x4x4 slice. The times are simulated.
128 devices in a mesh: ctx: 32 (over x, z, y_hi), head: 4 (over y_lo, core).
Axes of the slice: x: 4, y: 4 (y_hi: 2, y_lo: 2; y = y_hi * 2 + y_lo), z: 4, core: 2. Of those that a mesh axis runs over, the one named last changes fastest.
Arguments:
- query: bfloat16 [16384, 8192], P(('ctx', 'head')), may hold values from -6 to 6
- key: bfloat16 [16384, 1024], P(('ctx', 'head')), may hold values from -12 to 12
- value: bfloat16 [16384, 1024], P(('ctx', 'head')), may hold values from -6 to 6
- grad_out: bfloat16 [16384, 8192], P(('ctx', 'head')), may hold values from -6 to 6
- advantage: float32 [16384], P(('ctx', 'head')), may hold values from -3 to 3
- place: int32 [16384], replicated, may hold values from 0 to 16383, as said below
- segment: int32 [16384], replicated, may hold values from 0 to 93, as said below
Outputs:
- grad_query: bfloat16 [16384, 8192], P(('ctx', 'head'))
- grad_key: bfloat16 [16384, 1024], P(('ctx', 'head'))
- grad_value: bfloat16 [16384, 1024], P(('ctx', 'head'))
Inputs may be any that keep to these rules, and one draw needn't show every extreme that they name: place is a permutation; each aligned block of 128 tokens sends exactly 4 tokens to each aligned block of 512 positions. segment never falls along positions and starts at 0; each document holds 2 to 512 positions, and one holds exactly 512.
All inputs are finite; a program needn't handle non-finite values.
Results may differ from a plain program's by a relative error of at most 0.0066.
Values may be sent and summed in bfloat16 or wider, within the bound.
No kernel may reach another device: no remote copies, remote signals or barrier semaphores. Data moves between devices by JAX's collectives and lax.ppermute only.
A program may use at most 128 MiB of HBM per device.

v0:
```python
import math

import jax
import jax.numpy as jnp
from jax import lax
from jax.sharding import PartitionSpec as P

QUERY_HEADS = 64
KEY_VALUE_HEADS = 8
HEAD_SIZE = 128


NEG = -1e30


def passed_along(block, axis, distance):
    devices = range(lax.axis_size(axis))
    route = [(i - distance, i) for i in devices if i - distance in devices]
    return lax.ppermute(block, axis, route)


def block_visible(query_place, query_doc, key_place, key_doc):
    return (query_doc[:, None] == key_doc[None, :]) & (key_place[None, :] <= query_place[:, None])


def doc_of(segment, places, total, missing):
    inside = (places >= 0) & (places < total)
    return jnp.where(inside, segment[jnp.clip(places, 0, total - 1)], missing)


def block_scores(query_heads, keys_here):
    return jnp.einsum(
        "kgqd,ksd->kgqs", query_heads, keys_here, preferred_element_type=jnp.float32
    ) * HEAD_SIZE ** (-0.5)


def score_grads(side, keys_here, values_here, visible):
    query_heads, grad_heads, query_place, query_doc, row_lse, row_delta = side
    prob = jnp.where(
        visible, jnp.exp(block_scores(query_heads, keys_here) - row_lse[..., None]), 0.0
    )
    dprob = jnp.einsum(
        "kgqd,ksd->kgqs", grad_heads, values_here, preferred_element_type=jnp.float32
    )
    return (
        prob,
        (prob * (dprob - row_delta[..., None]) * HEAD_SIZE ** (-0.5)).astype(jnp.bfloat16),
    )


def pass_step(side):
    query_heads, grad_heads, query_place, query_doc, row_lse, row_delta = side

    def step(running, blockin):
        keys_here, values_here, place_here, doc_here = blockin
        visible = block_visible(query_place, query_doc, place_here, doc_here)
        summed = running
        prob, score_gradient = score_grads(side, keys_here, values_here, visible)
        summed = summed + jnp.einsum(
            "kgqs,ksd->kgqd", score_gradient, keys_here, preferred_element_type=jnp.float32
        )
        value_grad = jnp.einsum(
            "kgqs,kgqd->ksd",
            prob.astype(jnp.bfloat16),
            grad_heads,
            preferred_element_type=jnp.float32,
        )
        key_grad = jnp.einsum(
            "kgqs,kgqd->ksd", score_gradient, query_heads, preferred_element_type=jnp.float32
        )
        return (summed, jnp.stack([key_grad, value_grad]))

    return step


def to_rows(stacked):
    count, pair, heads, rows, size = stacked.shape
    return jnp.transpose(stacked, (0, 3, 1, 2, 4)).reshape(count * rows, pair * heads * size)


def head_major(rows, local_key_value, group_width):
    return jnp.transpose(
        rows.reshape(rows.shape[0], local_key_value, group_width, HEAD_SIZE), (1, 2, 0, 3)
    )


def shards(query, key, value, grad_out, advantage, place, segment):
    ctx_count = lax.axis_size("ctx")
    head_total = lax.axis_size("head")
    src_rows = query.shape[0]
    token_per_device = src_rows * head_total
    every_token = token_per_device * ctx_count
    ctx_id = lax.axis_index("ctx")
    local_key_value = KEY_VALUE_HEADS // head_total
    group_width = QUERY_HEADS // KEY_VALUE_HEADS
    kv_cols = local_key_value * HEAD_SIZE
    weighted = (advantage[:, None] * grad_out.astype(jnp.float32)).astype(jnp.bfloat16)
    sent = src_rows // ctx_count
    source = ctx_id * head_total + lax.axis_index("head")
    dest_all = (place // token_per_device).reshape(ctx_count * head_total, src_rows)
    onehot = (dest_all[:, :, None] == jnp.arange(ctx_count, dtype=jnp.int32)[None, None, :]).astype(
        jnp.int32
    )
    rank_all = jnp.sum(jnp.cumsum(onehot, axis=1) * onehot, axis=2) - 1
    own_dest = lax.dynamic_index_in_dim(dest_all, source, 0, keepdims=False)
    own_rank = lax.dynamic_index_in_dim(rank_all, source, 0, keepdims=False)
    slot_index = own_dest * sent + own_rank
    send_order = (
        jnp.zeros((src_rows,), jnp.int32).at[slot_index].set(jnp.arange(src_rows, dtype=jnp.int32))
    )

    def to_slots(rows):
        return rows[send_order].reshape(ctx_count, sent, rows.shape[1])

    arrived = (
        lax.all_to_all(
            lax.all_to_all(to_slots(query), "ctx", split_axis=0, concat_axis=0, tiled=True),
            "head",
            split_axis=2,
            concat_axis=1,
            tiled=True,
        ),
        lax.all_to_all(
            lax.all_to_all(to_slots(key), "ctx", split_axis=0, concat_axis=0, tiled=True),
            "head",
            split_axis=2,
            concat_axis=1,
            tiled=True,
        ),
        lax.all_to_all(
            lax.all_to_all(to_slots(value), "ctx", split_axis=0, concat_axis=0, tiled=True),
            "head",
            split_axis=2,
            concat_axis=1,
            tiled=True,
        ),
        lax.all_to_all(
            lax.all_to_all(to_slots(weighted), "ctx", split_axis=0, concat_axis=0, tiled=True),
            "head",
            split_axis=2,
            concat_axis=1,
            tiled=True,
        ),
    )
    tok_of_pos = (
        jnp.zeros((every_token,), jnp.int32).at[place].set(jnp.arange(every_token, dtype=jnp.int32))
    )
    own_tokens = lax.dynamic_slice_in_dim(tok_of_pos, ctx_id * token_per_device, token_per_device)
    recv_index = own_tokens // src_rows * sent + rank_all.reshape(every_token)[own_tokens]
    query_rows = arrived[0].reshape(token_per_device, arrived[0].shape[2])[recv_index]
    key_rows = arrived[1].reshape(token_per_device, arrived[1].shape[2])[recv_index]
    value_rows = arrived[2].reshape(token_per_device, arrived[2].shape[2])[recv_index]
    grad_rows = arrived[3].reshape(token_per_device, arrived[3].shape[2])[recv_index]
    prev_keys, prev_values = passed_along((key_rows, value_rows), "ctx", 1)
    keys_window = jnp.concatenate([prev_keys, key_rows], axis=0)
    values_window = jnp.concatenate([prev_values, value_rows], axis=0)
    own_start = ctx_id * token_per_device
    query_place = own_start + jnp.arange(token_per_device, dtype=jnp.int32)
    key_place = own_start - token_per_device + jnp.arange(2 * token_per_device, dtype=jnp.int32)
    query_doc = doc_of(segment, query_place, every_token, -1)
    key_doc = doc_of(segment, key_place, every_token, -2)
    query_heads = head_major(query_rows, local_key_value, group_width)
    grad_heads = head_major(grad_rows, local_key_value, group_width)
    key_block = math.gcd(token_per_device, 256)
    block_count = 2 * token_per_device // key_block

    def key_blocks(window):
        return jnp.transpose(
            window.reshape(block_count, key_block, local_key_value, HEAD_SIZE), (0, 2, 1, 3)
        )

    blocks = (
        key_blocks(keys_window),
        key_blocks(values_window),
        key_place.reshape(block_count, key_block),
        key_doc.reshape(block_count, key_block),
    )

    def stats_step(running, blockin):
        keys_here, values_here, place_here, doc_here = blockin
        visible = block_visible(query_place, query_doc, place_here, doc_here)
        row_high, row_total = running
        masked = jnp.where(visible, block_scores(query_heads, keys_here), NEG)
        new_high = jnp.maximum(row_high, jnp.max(masked, axis=-1))
        fresh = jnp.sum(jnp.where(visible, jnp.exp(masked - new_high[..., None]), 0.0), axis=-1)
        return ((new_high, row_total * jnp.exp(row_high - new_high) + fresh), None)

    start_high = jnp.full((local_key_value, group_width, token_per_device), NEG, jnp.float32)
    start_total = jnp.zeros((local_key_value, group_width, token_per_device), jnp.float32)
    (row_high, row_total), unused = lax.scan(stats_step, (start_high, start_total), blocks)
    row_lse = row_high + jnp.log(row_total)

    def output_step(running, blockin):
        keys_here, values_here, place_here, doc_here = blockin
        visible = block_visible(query_place, query_doc, place_here, doc_here)
        prob = jnp.where(
            visible, jnp.exp(block_scores(query_heads, keys_here) - row_lse[..., None]), 0.0
        )
        return (
            running
            + jnp.einsum(
                "kgqs,ksd->kgqd",
                prob.astype(jnp.bfloat16),
                values_here,
                preferred_element_type=jnp.float32,
            ),
            None,
        )

    start_grad = jnp.zeros((local_key_value, group_width, token_per_device, HEAD_SIZE), jnp.float32)
    attended, unused = lax.scan(output_step, start_grad, blocks)
    row_delta = jnp.sum(grad_heads.astype(jnp.float32) * attended, axis=-1)
    own_side = (query_heads, grad_heads, query_place, query_doc, row_lse, row_delta)
    query_grad, window_grads = lax.scan(pass_step(own_side), start_grad, blocks)
    window_grads = to_rows(window_grads)
    returned = passed_along(window_grads[:token_per_device].astype(jnp.bfloat16), "ctx", -1).astype(
        jnp.float32
    )
    summed_keys = window_grads[token_per_device:] + returned
    grad_query_rows = (
        jnp.transpose(query_grad, (2, 0, 1, 3))
        .reshape(token_per_device, local_key_value * group_width * HEAD_SIZE)
        .astype(jnp.bfloat16)
    )
    grad_key_rows = summed_keys[:, :kv_cols].astype(jnp.bfloat16)
    grad_value_rows = summed_keys[:, kv_cols:].astype(jnp.bfloat16)
    recv_inverse = (
        jnp.zeros((token_per_device,), jnp.int32)
        .at[recv_index]
        .set(jnp.arange(token_per_device, dtype=jnp.int32))
    )

    def to_sources(rows):
        return rows[recv_inverse].reshape(ctx_count, head_total * sent, rows.shape[1])

    back_query, back_key, back_value = (
        lax.all_to_all(
            lax.all_to_all(
                to_sources(grad_query_rows), "ctx", split_axis=0, concat_axis=0, tiled=True
            ),
            "head",
            split_axis=1,
            concat_axis=2,
            tiled=True,
        ),
        lax.all_to_all(
            lax.all_to_all(
                to_sources(grad_key_rows), "ctx", split_axis=0, concat_axis=0, tiled=True
            ),
            "head",
            split_axis=1,
            concat_axis=2,
            tiled=True,
        ),
        lax.all_to_all(
            lax.all_to_all(
                to_sources(grad_value_rows), "ctx", split_axis=0, concat_axis=0, tiled=True
            ),
            "head",
            split_axis=1,
            concat_axis=2,
            tiled=True,
        ),
    )
    out_query = back_query.reshape(src_rows, back_query.shape[2])[slot_index]
    out_key = back_key.reshape(src_rows, back_key.shape[2])[slot_index]
    out_value = back_value.reshape(src_rows, back_value.shape[2])[slot_index]
    return (out_query, out_key, out_value)


def solution(mesh):
    in_specs = (
        P(("ctx", "head"), None),
        P(("ctx", "head"), None),
        P(("ctx", "head"), None),
        P(("ctx", "head"), None),
        P(("ctx", "head")),
        P(),
        P(),
    )
    out_specs = (P(("ctx", "head"), None), P(("ctx", "head"), None), P(("ctx", "head"), None))
    return jax.shard_map(shards, mesh=mesh, in_specs=in_specs, out_specs=out_specs, check_vma=False)
```

profile of v0, /device:TPU:1, one launch (start us, length us, event | category | flops | bytes accessed | tf_op | source)
XLA Modules:
  0.0 622.1 jit_solution(4173449192302257205)
XLA Ops:
  5.7 11.3 %all-to-all-start = ((bf16[32,4,1024]{2,1,0:T(4,128)(2,1)}), bf16[32,4,1024]{2,1,0:T(4,128)(2,1)S(1)}, u32[]{:S(2)}, u32[]{:S(2)}) async-start(bf16[32,4,1024]{2,1,0:T(4,128)(2,1)} %reshape.168), calls=%async_computation | async-start | bytes 524288 | tf_op jit(solution)/shard_map/all_to_all | solution.py:124
  18.7 7.9 %all-to-all-done = bf16[32,4,1024]{2,1,0:T(4,128)(2,1)S(1)} async-done(((bf16[32,4,1024]{2,1,0:T(4,128)(2,1)}), bf16[32,4,1024]{2,1,0:T(4,128)(2,1)S(1)}, u32[]{:S(2)}, u32[]{:S(2)}) %all-to-all-start) | async-done | bytes 262176 | tf_op jit(solution)/shard_map/all_to_all | solution.py:124
  41.5 6.8 %all-to-all-start.1 = ((bf16[4,2,16384]{2,1,0:T(2,128)(2,1)}), bf16[4,2,16384]{2,1,0:T(2,128)(2,1)S(1)}, u32[]{:S(2)}, u32[]{:S(2)}) async-start(bf16[4,2,16384]{2,1,0:T(2,128)(2,1)} %reshape.374), calls=%async_computation.1 | async-start | bytes 524288 | tf_op jit(solution)/shard_map/all_to_all | solution.py:123
  61.0 7.0 %gather_fusion.9 = bf16[128,8192]{1,0:T(8,128)(2,1)} fusion(bf16[128,8192]{1,0:T(8,128)(2,1)} %multiply_convert_fusion, s32[1024]{0:T(1024)S(1)} %pad_clamp_fusion.4), kind=kCustom, calls=%fused_computation.9 | custom fusion | bytes 4194816 | tf_op jit(solution)/shard_map/gather | solution.py:113
  84.5 22.4 %all-to-all-done.6 = bf16[32,4,8192]{2,1,0:T(4,128)(2,1)} async-done(((bf16[32,4,8192]{2,1,0:T(4,128)(2,1)}), bf16[32,4,8192]{2,1,0:T(4,128)(2,1)}, u32[]{:S(2)}, u32[]{:S(2)}) %all-to-all-start.6) | async-done | bytes 2097184 | tf_op jit(solution)/shard_map/all_to_all | solution.py:138
  106.9 6.7 %all-to-all-start.2 = ((bf16[32,4,8192]{2,1,0:T(4,128)(2,1)}), bf16[32,4,8192]{2,1,0:T(4,128)(2,1)S(1)}, u32[]{:S(2)}, u32[]{:S(2)}) async-start(bf16[32,4,8192]{2,1,0:T(4,128)(2,1)} %reshape.171), calls=%async_computation.2 | async-start | bytes 4194304 | tf_op jit(solution)/shard_map/all_to_all | solution.py:117
  113.6 13.3 %copy.105 = bf16[32,4,8192]{0,1,2:T(4,128)(2,1)} copy(bf16[32,4,8192]{2,1,0:T(4,128)(2,1)} %all-to-all-done.6) | data formatting | bytes 4194304 | tf_op jit(solution)/shard_map/all_to_all | solution.py:138
  126.9 10.5 %reshape.380 = bf16[4,2,131072]{2,1,0:T(2,128)(2,1)} reshape(bf16[8192,4,32]{2,1,0:T(4,128)(2,1)} %bitcast.217) | data formatting | bytes 4194304
  141.2 7.9 %all-to-all-start.7 = ((bf16[4,2,131072]{2,1,0:T(2,128)(2,1)}), bf16[4,2,131072]{2,1,0:T(2,128)(2,1)}, u32[]{:S(2)}, u32[]{:S(2)}) async-start(bf16[4,2,131072]{2,1,0:T(2,128)(2,1)} %reshape.380), calls=%async_computation.7 | async-start | bytes 4194304 | tf_op jit(solution)/shard_map/all_to_all | solution.py:137
  149.2 60.3 %scatter_custom_fusion.1 = s32[16384]{0:T(1024)S(1)} fusion(s32[16384]{0:T(1024)S(1)} %get-tuple-element.364, s32[16384]{0:T(1024)S(1)} %iota.48, s32[]{:T(128)} %constant.111.clone.1), kind=kCustom, calls=%fused_computation.114 | custom fusion | bytes 65540 | tf_op jit(solution)/shard_map/scatter | solution.py:146
  209.6 9.3 %copy.99 = bf16[32,4,8192]{0,1,2:T(4,128)(2,1)} copy(bf16[32,4,8192]{2,1,0:T(4,128)(2,1)S(1)} %all-to-all-done.2) | data formatting | bytes 4194304 | tf_op jit(solution)/shard_map/all_to_all | solution.py:117
  218.9 10.5 %reshape.376 = bf16[4,2,131072]{2,1,0:T(2,128)(2,1)} reshape(bf16[8192,4,32]{2,1,0:T(4,128)(2,1)} %bitcast.218) | data formatting | bytes 4194304
  268.6 7.4 %reshape.381 = bf16[8192,4,32]{2,1,0:T(4,128)(2,1)} reshape(bf16[4,2,131072]{2,1,0:T(2,128)(2,1)} %all-to-all-done.7) | data formatting | bytes 4194304
  276.1 13.2 %copy.106 = bf16[32,4,4,2048]{3,1,2,0:T(4,128)(2,1)} copy(bf16[32,4,4,2048]{0,1,3,2:T(4,128)(2,1)} %bitcast.219) | data formatting | bytes 4194304 | tf_op jit(solution)/shard_map/all_to_all | solution.py:137
  298.7 7.4 %reshape.377 = bf16[8192,4,32]{2,1,0:T(4,128)(2,1)} reshape(bf16[4,2,131072]{2,1,0:T(2,128)(2,1)} %all-to-all-done.3) | data formatting | bytes 4194304
  306.1 13.2 %copy.100 = bf16[32,4,4,2048]{3,1,2,0:T(4,128)(2,1)} copy(bf16[32,4,4,2048]{0,1,3,2:T(4,128)(2,1)} %bitcast.220) | data formatting | bytes 4194304 | tf_op jit(solution)/shard_map/all_to_all | solution.py:116
  330.1 38.0 %while.37 = (s32[]{:T(128)}, f32[2,8,512]{2,1,0:T(8,128)S(1)}, f32[2,8,512]{2,1,0:T(8,128)S(1)}, s32[512]{0:T(512)S(1)}, s32[4,256]{1,0:T(4,128)S(1)}, /*index=5...) while((s32[]{:T(128)}, f32[2,8,512]{2,1,0:T(8,128)S(1)}, ...), condition=%wide.region_7.8_spmd.clone, body=%wide.region_4.7_spmd.clone.sunk | while | flops 554082816 | bytes 19837060 | solution.py:190
  368.1 24.3 %while.38 = (s32[]{:T(128)}, f32[2,8,512,128]{3,2,1,0:T(8,128)}, s32[512]{0:T(512)S(1)}, s32[4,256]{1,0:T(4,128)S(1)}, s32[4,256]{1,0:T(4,128)S(1)}, /*index=5*/...) while((s32[]{:T(128)}, f32[2,8,512,128]{3,2,1,0:T(8,128)}, ...), condition=%wide.region_9.10_spmd.clone, body=%wide.region_8.9_spmd.clone.sunk | while | flops 1084621312 | bytes 11056263 | solution.py:211
  373.2 6.2 select_add_fusion.4
  396.5 65.3 %while.39 = (s32[]{:T(128)}, f32[2,8,512,128]{3,2,1,0:T(8,128)}, f32[4,2,2,256,128]{4,3,2,1,0:T(8,128)}, s32[512]{0:T(512)S(1)}, s32[4,256]{1,0:T(4,128)S(1)}, /...) while((s32[]{:T(128)}, f32[2,8,512,128]{3,2,1,0:T(8,128)}, ...), condition=%wide.region_12.13_spmd.clone, body=%wide.region_11.12_spmd.clone.sunk | while | flops 2710045184 | bytes 82162400 | solution.py:214
  421.3 7.2 %select_add_fusion.5 = f32[2,8,512,128]{3,2,1,0:T(8,128)} fusion(f32[2,8,512,128]{3,2,1,0:T(8,128)} %get-tuple-element.668, bf16[2,8,512,256]{2,3,1,0:T(8,128)(2,1)} %copy-done.3, pred[]{:T(512)S(6)} %compare.15, bf16[4,2,256,128]{3,2,1,0:T(8,128)(2,1)S(1)} %get-tuple-element.688, s32[]{:T(128)} %get-tuple-element.667), kind=kOutput, calls=%fused_computation.62.clone.1 | convolution fusion | flops 538968064 | bytes 12713989 | tf_op jit(solution)/shard_map/while/body/eval_jaxpr/kgqs,ksd->kgqd/dot_general | solution.py:59
  438.0 7.2 %select_add_fusion.5 = f32[2,8,512,128]{3,2,1,0:T(8,128)} fusion(f32[2,8,512,128]{3,2,1,0:T(8,128)} %get-tuple-element.668, bf16[2,8,512,256]{2,3,1,0:T(8,128)(2,1)} %copy-done.3, pred[]{:T(512)S(6)} %compare.15, bf16[4,2,256,128]{3,2,1,0:T(8,128)(2,1)S(1)} %get-tuple-element.688, s32[]{:T(128)} %get-tuple-element.667), kind=kOutput, calls=%fused_computation.62.clone.1 | convolution fusion | flops 538968064 | bytes 12713989 | tf_op jit(solution)/shard_map/while/body/eval_jaxpr/kgqs,ksd->kgqd/dot_general | solution.py:59
  454.6 7.2 %select_add_fusion.5 = f32[2,8,512,128]{3,2,1,0:T(8,128)} fusion(f32[2,8,512,128]{3,2,1,0:T(8,128)} %get-tuple-element.668, bf16[2,8,512,256]{2,3,1,0:T(8,128)(2,1)} %copy-done.3, pred[]{:T(512)S(6)} %compare.15, bf16[4,2,256,128]{3,2,1,0:T(8,128)(2,1)S(1)} %get-tuple-element.688, s32[]{:T(128)} %get-tuple-element.667), kind=kOutput, calls=%fused_computation.62.clone.1 | convolution fusion | flops 538968064 | bytes 12713989 | tf_op jit(solution)/shard_map/while/body/eval_jaxpr/kgqs,ksd->kgqd/dot_general | solution.py:59
  471.0 10.3 %collective-permute-done.2 = bf16[512,512]{1,0:T(8,128)(2,1)S(1)} collective-permute-done((bf16[512,512]{1,0:T(8,128)(2,1)S(1)}, bf16[512,512]{1,0:T(8,128)(2,1)S(1)}, u32[]{:S(2)}, u32[]{:S(2)}) %collective-permute-start.2) | collective-permute-done | bytes 524320 | tf_op jit(solution)/shard_map/ppermute | solution.py:19
  484.1 10.8 %all-to-all-start.12 = ((bf16[32,16,256]{2,1,0:T(8,128)(2,1)}), bf16[32,16,256]{2,1,0:T(8,128)(2,1)S(1)}, u32[]{:S(2)}, u32[]{:S(2)}) async-start(bf16[32,16,256]{2,1,0:T(8,128)(2,1)} %bitcast.25), calls=%async_computation.12 | async-start | bytes 524288 | tf_op jit(solution)/shard_map/all_to_all | solution.py:256
  497.5 7.1 %all-to-all-done.12 = bf16[32,16,256]{2,1,0:T(8,128)(2,1)S(1)} async-done(((bf16[32,16,256]{2,1,0:T(8,128)(2,1)}), bf16[32,16,256]{2,1,0:T(8,128)(2,1)S(1)}, u32[]{:S(2)}, u32[]{:S(2)}) %all-to-all-start.12) | async-done | bytes 262176 | tf_op jit(solution)/shard_map/all_to_all | solution.py:256
  509.2 8.9 %all-to-all-done.10 = bf16[32,16,256]{2,1,0:T(8,128)(2,1)S(1)} async-done(((bf16[32,16,256]{2,1,0:T(8,128)(2,1)}), bf16[32,16,256]{2,1,0:T(8,128)(2,1)S(1)}, u32[]{:S(2)}, u32[]{:S(2)}) %all-to-all-start.10) | async-done | bytes 262176 | tf_op jit(solution)/shard_map/all_to_all | solution.py:247
  518.2 7.1 %all-to-all-start.13 = ((bf16[32,16,256]{2,0,1:T(8,128)(2,1)}), bf16[32,16,256]{2,0,1:T(8,128)(2,1)S(1)}, u32[]{:S(2)}, u32[]{:S(2)}) async-start(bf16[32,16,256]{2,0,1:T(8,128)(2,1)} %copy.115), calls=%async_computation.13 | async-start | bytes 524288 | tf_op jit(solution)/shard_map/all_to_all | solution.py:255
  537.8 28.9 %all-to-all-done.8 = bf16[32,16,2048]{2,1,0:T(8,128)(2,1)S(1)} async-done(((bf16[32,16,2048]{2,1,0:T(8,128)(2,1)}), bf16[32,16,2048]{2,1,0:T(8,128)(2,1)S(1)}, u32[]{:S(2)}, u32[]{:S(2)}) %all-to-all-start.8) | async-done | bytes 2097184 | tf_op jit(solution)/shard_map/all_to_all | solution.py:238
  566.7 6.3 %all-to-all-start.11 = ((bf16[32,16,256]{2,0,1:T(8,128)(2,1)}), bf16[32,16,256]{2,0,1:T(8,128)(2,1)S(1)}, u32[]{:S(2)}, u32[]{:S(2)}) async-start(bf16[32,16,256]{2,0,1:T(8,128)(2,1)} %copy.113), calls=%async_computation.11 | async-start | bytes 524288 | tf_op jit(solution)/shard_map/all_to_all | solution.py:246
  587.4 21.2 %all-to-all-done.9 = bf16[32,16,2048]{2,0,1:T(8,128)(2,1)} async-done(((bf16[32,16,2048]{2,0,1:T(8,128)(2,1)}), bf16[32,16,2048]{2,0,1:T(8,128)(2,1)}, u32[]{:S(2)}, u32[]{:S(2)}) %all-to-all-start.9) | async-done | bytes 2097184 | tf_op jit(solution)/shard_map/all_to_all | solution.py:237
  614.6 7.1 %gather_fusion.12 = bf16[128,8192]{1,0:T(8,128)(2,1)} fusion(bf16[128,8192]{1,0:T(8,128)(2,1)} %bitcast.215, s32[1024]{0:T(1024)S(1)} %pad_clamp_fusion), kind=kCustom, calls=%fused_computation.12 | custom fusion | bytes 4194816 | tf_op jit(solution)/shard_map/gather | solution.py:265
  (235 shorter events, 268.7 us)
Async XLA Ops:
  0.6 76.5 %copy-start = (bf16[128,8192]{1,0:T(8,128)(2,1)S(1)}, bf16[128,8192]{1,0:T(8,128)(2,1)}, u32[]{:S(2)}) copy-start(bf16[128,8192]{1,0:T(8,128)(2,1)} %param.13) | copy-start | bytes 6291460
  0.6 3.4 copy-start.5
  0.7 16.4 %copy-start.6 = (bf16[128,1024]{1,0:T(8,128)(2,1)S(1)}, bf16[128,1024]{1,0:T(8,128)(2,1)}, u32[]{:S(2)}) copy-start(bf16[128,1024]{1,0:T(8,128)(2,1)} %param.15) | copy-start | bytes 786436
  5.7 20.9 %all-to-all-start = ((bf16[32,4,1024]{2,1,0:T(4,128)(2,1)}), bf16[32,4,1024]{2,1,0:T(4,128)(2,1)S(1)}, u32[]{:S(2)}, u32[]{:S(2)}) async-start(bf16[32,4,1024]{2,1,0:T(4,128)(2,1)} %reshape.168), calls=%async_computation | async-start | bytes 524288 | tf_op jit(solution)/shard_map/all_to_all | solution.py:124
  27.4 13.4 %all-to-all-start.4 = ((bf16[32,4,1024]{2,1,0:T(4,128)(2,1)}), bf16[32,4,1024]{2,1,0:T(4,128)(2,1)S(1)}, u32[]{:S(2)}, u32[]{:S(2)}) async-start(bf16[32,4,1024]{2,1,0:T(4,128)(2,1)} %reshape.174), calls=%async_computation.4 | async-start | bytes 524288 | tf_op jit(solution)/shard_map/all_to_all | solution.py:131
  34.7 23.0 %copy-start.11 = (f32[128]{0:T(128)S(1)}, f32[128]{0:T(128)}, u32[]{:S(2)}) copy-start(f32[128]{0:T(128)} %param.17) | copy-start | bytes 1540
  41.5 12.0 %all-to-all-start.1 = ((bf16[4,2,16384]{2,1,0:T(2,128)(2,1)}), bf16[4,2,16384]{2,1,0:T(2,128)(2,1)S(1)}, u32[]{:S(2)}, u32[]{:S(2)}) async-start(bf16[4,2,16384]{2,1,0:T(2,128)(2,1)} %reshape.374), calls=%async_computation.1 | async-start | bytes 524288 | tf_op jit(solution)/shard_map/all_to_all | solution.py:123
  53.4 18.7 %all-to-all-start.5 = ((bf16[4,2,16384]{2,1,0:T(2,128)(2,1)}), bf16[4,2,16384]{2,1,0:T(2,128)(2,1)S(1)}, u32[]{:S(2)}, u32[]{:S(2)}) async-start(bf16[4,2,16384]{2,1,0:T(2,128)(2,1)} %reshape.378), calls=%async_computation.5 | async-start | bytes 524288 | tf_op jit(solution)/shard_map/all_to_all | solution.py:130
  72.1 34.8 %all-to-all-start.6 = ((bf16[32,4,8192]{2,1,0:T(4,128)(2,1)}), bf16[32,4,8192]{2,1,0:T(4,128)(2,1)}, u32[]{:S(2)}, u32[]{:S(2)}) async-start(bf16[32,4,8192]{2,1,0:T(4,128)(2,1)} %reshape.177), calls=%async_computation.6 | async-start | bytes 4194304 | tf_op jit(solution)/shard_map/all_to_all | solution.py:138
  106.9 34.3 %all-to-all-start.2 = ((bf16[32,4,8192]{2,1,0:T(4,128)(2,1)}), bf16[32,4,8192]{2,1,0:T(4,128)(2,1)S(1)}, u32[]{:S(2)}, u32[]{:S(2)}) async-start(bf16[32,4,8192]{2,1,0:T(4,128)(2,1)} %reshape.171), calls=%async_computation.2 | async-start | bytes 4194304 | tf_op jit(solution)/shard_map/all_to_all | solution.py:117
  141.2 88.3 %all-to-all-start.7 = ((bf16[4,2,131072]{2,1,0:T(2,128)(2,1)}), bf16[4,2,131072]{2,1,0:T(2,128)(2,1)}, u32[]{:S(2)}, u32[]{:S(2)}) async-start(bf16[4,2,131072]{2,1,0:T(2,128)(2,1)} %reshape.380), calls=%async_computation.7 | async-start | bytes 4194304 | tf_op jit(solution)/shard_map/all_to_all | solution.py:137
  229.5 4.7 copy-start.2
  229.5 69.2 %all-to-all-start.3 = ((bf16[4,2,131072]{2,1,0:T(2,128)(2,1)}), bf16[4,2,131072]{2,1,0:T(2,128)(2,1)}, u32[]{:S(2)}, u32[]{:S(2)}) async-start(bf16[4,2,131072]{2,1,0:T(2,128)(2,1)} %reshape.376), calls=%async_computation.3 | async-start | bytes 4194304 | tf_op jit(solution)/shard_map/all_to_all | solution.py:116
  243.6 3.2 copy-start.10
  246.8 15.9 %collective-permute-start = (bf16[512,256]{1,0:T(8,128)(2,1)S(1)}, bf16[512,256]{1,0:T(8,128)(2,1)S(1)}, u32[]{:S(2)}, u32[]{:S(2)}) collective-permute-start(bf16[512,256]{1,0:T(8,128)(2,1)S(1)} %gather_fusion.4), channel_id=1, source_target_pairs={{0,4},{4,8},{8,12},{12,16},{16,20},{20,24},{24,28},{28,32},{32,36}... | collective-permute-start | bytes 786440 | tf_op jit(solution)/shard_map/ppermute | solution.py:19
  256.1 12.2 %collective-permute-start.1 = (bf16[512,256]{1,0:T(8,128)(2,1)S(1)}, bf16[512,256]{1,0:T(8,128)(2,1)S(1)}, u32[]{:S(2)}, u32[]{:S(2)}) collective-permute-start(bf16[512,256]{1,0:T(8,128)(2,1)S(1)} %gather_fusion.8), channel_id=1, source_target_pairs={{0,4},{4,8},{8,12},{12,16},{16,20},{20,24},{24,28},{28,32},{32,36}... | collective-permute-start | bytes 786440 | tf_op jit(solution)/shard_map/ppermute | solution.py:19
  325.1 2.4 copy-start.4
  401.3 2.0 copy-start.3
  412.1 1.6 copy-start.7
  416.7 2.0 copy-start.3
  428.8 1.6 copy-start.7
  433.3 2.0 copy-start.3
  450.0 2.0 copy-start.3
  463.9 17.4 %collective-permute-start.2 = (bf16[512,512]{1,0:T(8,128)(2,1)S(1)}, bf16[512,512]{1,0:T(8,128)(2,1)S(1)}, u32[]{:S(2)}, u32[]{:S(2)}) collective-permute-start(bf16[512,512]{1,0:T(8,128)(2,1)S(1)} %convert_element_type.46), channel_id=1, source_target_pairs={{4,0},{8,4},{12,8},{16,12},{20,16},{24,20},{28,24},{32,28},{36,32}... | collective-permute-start | bytes 1572872 | tf_op jit(solution)/shard_map/ppermute | solution.py:19
  484.1 20.5 %all-to-all-start.12 = ((bf16[32,16,256]{2,1,0:T(8,128)(2,1)}), bf16[32,16,256]{2,1,0:T(8,128)(2,1)S(1)}, u32[]{:S(2)}, u32[]{:S(2)}) async-start(bf16[32,16,256]{2,1,0:T(8,128)(2,1)} %bitcast.25), calls=%async_computation.12 | async-start | bytes 524288 | tf_op jit(solution)/shard_map/all_to_all | solution.py:256
  504.6 13.6 %all-to-all-start.10 = ((bf16[32,16,256]{2,1,0:T(8,128)(2,1)}), bf16[32,16,256]{2,1,0:T(8,128)(2,1)S(1)}, u32[]{:S(2)}, u32[]{:S(2)}) async-start(bf16[32,16,256]{2,1,0:T(8,128)(2,1)} %bitcast.22), calls=%async_computation.10 | async-start | bytes 524288 | tf_op jit(solution)/shard_map/all_to_all | solution.py:247
  518.2 14.8 %all-to-all-start.13 = ((bf16[32,16,256]{2,0,1:T(8,128)(2,1)}), bf16[32,16,256]{2,0,1:T(8,128)(2,1)S(1)}, u32[]{:S(2)}, u32[]{:S(2)}) async-start(bf16[32,16,256]{2,0,1:T(8,128)(2,1)} %copy.115), calls=%async_computation.13 | async-start | bytes 524288 | tf_op jit(solution)/shard_map/all_to_all | solution.py:255
  533.0 33.7 %all-to-all-start.8 = ((bf16[32,16,2048]{2,1,0:T(8,128)(2,1)}), bf16[32,16,2048]{2,1,0:T(8,128)(2,1)S(1)}, u32[]{:S(2)}, u32[]{:S(2)}) async-start(bf16[32,16,2048]{2,1,0:T(8,128)(2,1)} %bitcast.225), calls=%async_computation.8 | async-start | bytes 4194304 | tf_op jit(solution)/shard_map/all_to_all | solution.py:238
  566.7 11.3 %all-to-all-start.11 = ((bf16[32,16,256]{2,0,1:T(8,128)(2,1)}), bf16[32,16,256]{2,0,1:T(8,128)(2,1)S(1)}, u32[]{:S(2)}, u32[]{:S(2)}) async-start(bf16[32,16,256]{2,0,1:T(8,128)(2,1)} %copy.113), calls=%async_computation.11 | async-start | bytes 524288 | tf_op jit(solution)/shard_map/all_to_all | solution.py:246
  575.5 8.2 %copy-start.13 = (s32[128]{0:T(128)S(1)}, s32[128]{0:T(128)}, u32[]{:S(2)}) copy-start(s32[128]{0:T(128)} %copy-done.12) | copy-start | bytes 1540
  578.0 30.5 %all-to-all-start.9 = ((bf16[32,16,2048]{2,0,1:T(8,128)(2,1)}), bf16[32,16,2048]{2,0,1:T(8,128)(2,1)}, u32[]{:S(2)}, u32[]{:S(2)}) async-start(bf16[32,16,2048]{2,0,1:T(8,128)(2,1)} %copy.109), calls=%async_computation.9 | async-start | bytes 4194304 | tf_op jit(solution)/shard_map/all_to_all | solution.py:237
  614.6 7.1 %copy-start.1 = (bf16[128,8192]{1,0:T(8,128)(2,1)S(1)}, bf16[128,8192]{1,0:T(8,128)(2,1)}, u32[]{:S(2)}) copy-start(bf16[128,8192]{1,0:T(8,128)(2,1)} %param.13) | copy-start | bytes 6291460
  (5 other events, 5.6 us)
where the time goes:
time: 633 us; the launch traced here: 622 us
  local copies, waits for them, and re-layouts  259 us (41%)
  waiting for transfers between devices  129 us (20%)
  matrix products  99.2 us (16%)
  starting transfers between devices  96.7 us (15%)
  other arithmetic  36.3 us (6%)
    scatter x1, local copies, waits for them, and re-layouts, shards(): jnp.zeros((every_token,), jnp.int32).at[place]  60.3 us
    unnamed x38, local copies, waits for them, and re-layouts  51 us
    all_to_all x1, waiting for transfers between devices, shards(): lax.all_to_all(to_sources(grad_query_rows), 'ctx', split_axis=0, concat_a...  28.9 us
    dot_general x4, matrix products, step(): jnp.einsum('kgqs,ksd->kgqd', score_gradient, keys_here, preferred_element...  27.6 us
    dot_general x8, matrix products, block_scores(): jnp.einsum('kgqd,ksd->kgqs', query_heads, keys_here, preferred_element_ty...  24 us
    dot_general x4, matrix products, output_step(): jnp.einsum('kgqs,ksd->kgqd', prob.astype(jnp.bfloat16), values_here, pref...  23.3 us
    all_to_all x1, waiting for transfers between devices, shards(): lax.all_to_all(to_slots(weighted), 'ctx', split_axis=0, concat_axis=0, ti...  22.4 us
    all_to_all x1, waiting for transfers between devices, shards(): lax.all_to_all(lax.all_to_all(to_sources(grad_query_rows), 'ctx', split_a...  21.2 us
  transfers between devices with their start and end apart: 17, of which 13 were waited for; matrix products, arithmetic and copies ran while one was open for 33% of the time, Pallas kernels for 0%

commit v1 on v0

v1 whole, which is shorter than its diff:
```python
import functools

import jax
import jax.numpy as jnp
from jax import lax
from jax.experimental import pallas as pl
from jax.experimental.pallas import tpu as pltpu
from jax.sharding import PartitionSpec as P

GROUPS = 8
WIDTH = 8
D = 128
BLOCK = 512
PAIRS = 16
SCALE = D ** (-0.5)
LOG2E = 1.4426950408889634
NEG = -1e30
F32 = jnp.float32
BF16 = jnp.bfloat16

SEND_ROWS = 152
BACK_ROWS = 88
VMEM_LIMIT = 56 * 1024 * 1024


def iota(shape, dim):
    return lax.broadcasted_iota(jnp.int32, shape, dim)


def dot(a, b):
    return jnp.dot(a, b, preferred_element_type=F32)


def dot_nt(a, b):
    return lax.dot_general(a, b, (((1,), (1,)), ((), ())), preferred_element_type=F32)


def spread(row):
    square = jnp.broadcast_to(row.astype(F32), (128, 128))
    return square, jnp.transpose(square)


def token_codes(place_ref, me):
    row = place_ref[pl.ds(me, 1), :]
    dest = lax.shift_right_logical(row, 9)
    across, down = spread(dest)
    before = (across == down) & (iota((128, 128), 0) < iota((128, 128), 1))
    rank = jnp.sum(before.astype(F32), axis=0, keepdims=True).astype(jnp.int32)
    return lax.shift_right_logical(dest, 1), dest & 1, rank


def row_codes(pair, half, rank, per_pair):
    first = jnp.where(half == 0, pair * per_pair + rank, -1000)
    second = jnp.where(half == 1, pair * per_pair + rank, -1000)
    halo = jnp.where((half == 1) & (pair < PAIRS - 1), (pair + 1) * per_pair + rank, -1000)
    return first, second, halo


def onehot(index, code):
    return (index == code).astype(F32).astype(BF16)


def send_kernel(me_ref, place_ref, adv_ref, q_ref, k_ref, v_ref, g_ref, out_ref, t1, t2, t3, t4, adv):
    @pl.when(pl.program_id(0) == 0)
    def _():
        pair, half, rank = token_codes(place_ref, me_ref[0])
        first, second, halo = row_codes(pair, half, rank, 16)
        rows = iota((256, 128), 0)
        for j in range(4):
            cols = slice(j * 128, (j + 1) * 128)
            t1[:, cols] = onehot(rows, first + 4 * j)
            t2[:, cols] = onehot(rows, second + 4 * j)
            t3[:, cols] = onehot(rows, (halo if j < 2 else first) + 4 * j)
        second8 = row_codes(pair, half, rank, 8)[1]
        rows8 = iota((128, 128), 0)
        for j in range(2):
            t4[:, j * 128 : (j + 1) * 128] = onehot(rows8, second8 + 4 * j)
        adv[...] = jnp.transpose(jnp.broadcast_to(adv_ref[...], (128, 128)))

    weight = adv[...]
    grad = jnp.concatenate(
        [
            (g_ref[:, h * 128 : (h + 1) * 128].astype(F32) * weight).astype(BF16)
            for h in range(WIDTH)
        ],
        axis=1,
    )
    for at, block in ((0, q_ref[...]), (64, grad)):
        stacked = jnp.concatenate([block[:, j * 256 : (j + 1) * 256] for j in range(4)], axis=0)
        for b, t in enumerate((t1, t2)):
            moved = dot(t[...], stacked).astype(BF16)
            start = at + 32 * b
            out_ref[:, 0, start : start + 16, :] = moved[:, :128].reshape(PAIRS, 16, 128)
            out_ref[:, 0, start + 16 : start + 32, :] = moved[:, 128:].reshape(PAIRS, 16, 128)
    k, v = k_ref[...], v_ref[...]
    moved = dot(t3[...], jnp.concatenate([k, v, k, v], axis=0)).astype(BF16)
    out_ref[:, 0, 128:144, :] = moved.reshape(PAIRS, 16, 128)
    moved = dot(t4[...], jnp.concatenate([k, v], axis=0)).astype(BF16)
    out_ref[:, 0, 144:152, :] = moved.reshape(PAIRS, 8, 128)


def source_maps(place_ref, block, spread_ref, gather_ref):
    place = place_ref[...]
    own = lax.shift_right_logical(place, 9) == block
    local = (place - block * BLOCK + 1).astype(F32)
    member = own.astype(F32)
    lower = (iota((128, 128), 0) < iota((128, 128), 1)).astype(F32).astype(BF16)
    rank = dot(member.astype(BF16), lower)
    picked = jnp.where(own, local, 0.0)
    member_t, picked_t = jnp.transpose(member), jnp.transpose(picked)
    upper = (iota((128, 128), 1) < iota((128, 128), 0)).astype(F32).astype(BF16)
    rank_t = dot(upper, member_t.astype(BF16))
    for r in range(4):
        col = jnp.sum(jnp.where(rank == r, picked, 0.0), axis=1, keepdims=True) - 1.0
        row = jnp.sum(jnp.where(rank_t == r, picked_t, 0.0), axis=0, keepdims=True) - 1.0
        at = slice(r * 128, (r + 1) * 128)
        spread_ref[:, at] = onehot(iota((BLOCK, 128), 0), row.astype(jnp.int32))
        gather_ref[at, :] = onehot(iota((128, BLOCK), 1), col.astype(jnp.int32))


def attend_kernel(
    me_ref, seg_ref, place_ref, doc_ref, in_ref, out_ref,
    to_pos, to_src, stage, qs, ws, ks, vs, kt, doc_t, s_scr, p_scr, dq_acc, dq_t, dk_acc, dv_acc,
):
    pair = lax.shift_right_logical(me_ref[0], 3)

    for b in range(3):
        source_maps(place_ref, 2 * pair - 1 + b, to_pos.at[b], to_src.at[b])

    def unpacked(start, rows):
        block = in_ref[:, start : start + rows, :].astype(F32)
        stage[0 : 128 * rows, :] = block.reshape(128 * rows, 128)
        return [
            jnp.concatenate(
                [stage[pl.ds(4 * j + r, 128, stride=rows), :].astype(BF16) for r in range(4)], axis=0
            )
            for j in range(rows // 4)
        ]

    for at, target in ((0, qs), (64, ws)):
        for b in range(2):
            left = unpacked(at + 32 * b, 16)
            right = unpacked(at + 32 * b + 16, 16)
            for j in range(4):
                both = jnp.concatenate([left[j], right[j]], axis=1)
                moved = dot(to_pos[b + 1], both).astype(BF16)
                target[2 * j, b * BLOCK : (b + 1) * BLOCK, :] = moved[:, :128]
                target[2 * j + 1, b * BLOCK : (b + 1) * BLOCK, :] = moved[:, 128:]
    kv = unpacked(128, 16) + unpacked(144, 8)
    for b in range(3):
        moved = dot(to_pos[b], jnp.concatenate(kv[2 * b : 2 * b + 2], axis=1)).astype(BF16)
        ks[b * BLOCK : (b + 1) * BLOCK, :] = moved[:, :128]
        vs[b * BLOCK : (b + 1) * BLOCK, :] = moved[:, 128:]
    eye = onehot(iota((128, 128), 0), iota((128, 128), 1))
    kt[...] = dot_nt(eye, ks[...]).astype(BF16)
    for b in range(12):
        at = jnp.maximum(8 * pair - 4 + b, 0)
        doc_t[b] = jnp.transpose(jnp.broadcast_to(doc_ref[pl.ds(at, 1), :].astype(F32), (128, 128)))
    dk_acc[...] = jnp.zeros_like(dk_acc)
    dv_acc[...] = jnp.zeros_like(dv_acc)

    causal = iota((128, 128), 0) - iota((128, 128), 1)

    def query_block(ib, carry):
        block = 8 * pair + ib
        first_doc = seg_ref[block * 128]
        count = jnp.int32(1)
        for back in range(1, 5):
            other = jnp.maximum(block - back, 0)
            near = (block >= back) & (seg_ref[other * 128 + 127] >= first_doc)
            count = count + near.astype(jnp.int32)
        query_doc = doc_ref[pl.ds(block, 1), :].astype(F32)
        rows = pl.ds(pl.multiple_of(ib * 128, 128), 128)

        def key_rows(t):
            return pl.ds(pl.multiple_of((ib + 4 - t) * 128, 128), 128)

        def scores(t, high):
            keys = ks[key_rows(t), :]
            seen = (doc_t[ib + 4 - t] == query_doc) & (causal <= t * 128)
            bias = jnp.where(seen, 0.0, NEG)
            new = []
            for h in range(WIDTH):
                part = dot_nt(keys, qs[h, rows, :]) * (SCALE * LOG2E) + bias
                s_scr[t, h] = part
                new.append(jnp.maximum(high[h], jnp.max(part.reshape(16, 8, 128), axis=0)))
            return tuple(new)

        high = lax.fori_loop(0, count, scores, (jnp.full((8, 128), NEG, F32),) * WIDTH)
        high = [jnp.max(x, axis=0, keepdims=True) for x in high]

        def sums(t, carry):
            total, delta = carry
            values = vs[key_rows(t), :]
            new_total, new_delta = [], []
            for h in range(WIDTH):
                prob = jnp.exp2(s_scr[t, h] - high[h])
                dprob = dot_nt(values, ws[h, rows, :])
                s_scr[t, h] = prob
                p_scr[t, h] = dprob
                new_total.append(total[h] + jnp.sum(prob.reshape(16, 8, 128), axis=0))
                new_delta.append(delta[h] + jnp.sum((prob * dprob).reshape(16, 8, 128), axis=0))
            return tuple(new_total), tuple(new_delta)

        zero = (jnp.zeros((8, 128), F32),) * WIDTH
        total, delta = lax.fori_loop(0, count, sums, (zero, zero))
        inverse = [1.0 / jnp.sum(x, axis=0, keepdims=True) for x in total]
        delta = [jnp.sum(x, axis=0, keepdims=True) * i for x, i in zip(delta, inverse)]
        dq_acc[...] = jnp.zeros_like(dq_acc)

        def grads(t, carry):
            weights, dscore = [], []
            for h in range(WIDTH):
                prob = s_scr[t, h] * inverse[h]
                weights.append(prob.astype(BF16))
                dscore.append((prob * (p_scr[t, h] - delta[h])).astype(BF16))
            weights = jnp.concatenate(weights, axis=1)
            dscore = jnp.concatenate(dscore, axis=1)
            at = key_rows(t)
            grad_rows = jnp.concatenate([ws[h, rows, :] for h in range(WIDTH)], axis=0)
            query_rows = jnp.concatenate([qs[h, rows, :] for h in range(WIDTH)], axis=0)
            dv_acc[at, :] += dot(weights, grad_rows)
            dk_acc[at, :] += dot(dscore, query_rows)
            dq_acc[...] += dot(kt[:, at], dscore)
            return carry

        lax.fori_loop(0, count, grads, 0)
        for h in range(WIDTH):
            dq_t[h, :, rows] = (dq_acc[:, h * 128 : (h + 1) * 128] * SCALE).astype(BF16)
        return carry

    lax.fori_loop(0, 8, query_block, 0)

    def packed(start, parts):
        rows = 4 * len(parts)
        for j, part in enumerate(parts):
            for r in range(4):
                stage[pl.ds(4 * j + r, 128, stride=rows), :] = part[r * 128 : (r + 1) * 128]
        out_ref[:, start : start + rows, :] = (
            stage[0 : 128 * rows, :].astype(BF16).reshape(128, rows, 128)
        )

    for b in range(2):
        for q in range(2):
            parts = [
                dot_nt(to_src[b + 1], dq_t[2 * j + q, :, b * BLOCK : (b + 1) * BLOCK])
                for j in range(4)
            ]
            packed(32 * b + 16 * q, parts)
    kv = []
    for b in range(3):
        at = slice(b * BLOCK, (b + 1) * BLOCK)
        for part in ((dk_acc[at, :] * SCALE).astype(BF16), dv_acc[at, :].astype(BF16)):
            kv.append(dot(to_src[b], part))
    packed(64, kv[:4])
    packed(80, kv[4:])


def return_kernel(me_ref, place_ref, in_ref, dq_ref, dk_ref, dv_ref, u1, uk, uv):
    @pl.when(pl.program_id(0) == 0)
    def _():
        pair, half, rank = token_codes(place_ref, me_ref[0])

        def column(code):
            return spread(code)[1].astype(jnp.int32)

        first, second, halo = [column(c) for c in row_codes(pair, half, rank, 16)]
        second8 = column(row_codes(pair, half, rank, 8)[1])
        for at in range(2):
            lanes = iota((128, 128), 1) + 128 * at
            for j in range(4):
                rows = slice(j * 128, (j + 1) * 128)
                u1[rows, at * 128 : (at + 1) * 128] = onehot(lanes, first + 4 * j)
                u1[rows, 256 + at * 128 : 256 + (at + 1) * 128] = onehot(lanes, second + 4 * j)
            for j, u in enumerate((uk, uv)):
                u[:, at * 128 : (at + 1) * 128] = onehot(lanes, halo + 4 * j) + onehot(
                    lanes, first + 8 + 4 * j
                )
        for j, u in enumerate((uk, uv)):
            u[:, 256:384] = onehot(iota((128, 128), 1), second8 + 4 * j)

    def flat(start, rows):
        return in_ref[:, 0, start : start + rows, :].reshape(PAIRS * rows, 128)

    both = jnp.concatenate(
        [jnp.concatenate([flat(32 * b + 16 * q, 16) for q in range(2)], axis=1) for b in range(2)],
        axis=0,
    )
    moved = dot(u1[...], both).astype(BF16)
    for j in range(4):
        dq_ref[:, j * 256 : (j + 1) * 256] = moved[j * 128 : (j + 1) * 128, :]
    kv = jnp.concatenate([flat(64, 16), flat(80, 8)], axis=0)
    dk_ref[...] = dot(uk[...], kv).astype(BF16)
    dv_ref[...] = dot(uv[...], kv).astype(BF16)


def shards(query, key, value, grad_out, advantage, place, segment):
    me = (lax.axis_index("ctx") * 4 + lax.axis_index("head")).astype(jnp.int32).reshape(1)
    place2 = place.reshape(128, 128)
    doc2 = segment.reshape(128, 128)
    smem = pl.BlockSpec(memory_space=pltpu.SMEM)
    vmem = pl.BlockSpec(memory_space=pltpu.VMEM)
    whole = pl.BlockSpec((128, 128), lambda g: (0, 0))
    params = pltpu.CompilerParams(vmem_limit_bytes=VMEM_LIMIT)

    sent = pl.pallas_call(
        send_kernel,
        grid=(GROUPS,),
        in_specs=[
            smem,
            whole,
            pl.BlockSpec((1, 128), lambda g: (0, 0)),
            pl.BlockSpec((128, WIDTH * D), lambda g: (0, g)),
            pl.BlockSpec((128, D), lambda g: (0, g)),
            pl.BlockSpec((128, D), lambda g: (0, g)),
            pl.BlockSpec((128, WIDTH * D), lambda g: (0, g)),
        ],
        out_specs=pl.BlockSpec((PAIRS, 1, SEND_ROWS, 128), lambda g: (0, g, 0, 0)),
        out_shape=jax.ShapeDtypeStruct((PAIRS, GROUPS, SEND_ROWS, 128), BF16),
        scratch_shapes=[
            pltpu.VMEM((256, 512), BF16),
            pltpu.VMEM((256, 512), BF16),
            pltpu.VMEM((256, 512), BF16),
            pltpu.VMEM((128, 256), BF16),
            pltpu.VMEM((128, 128), F32),
        ],
        compiler_params=params,
        name="to_blocks",
    )(me, place2, advantage.reshape(1, 128), query, key, value, grad_out)

    arrived = lax.all_to_all(
        sent.reshape(128, SEND_ROWS, 128), ("ctx", "head"), split_axis=0, concat_axis=0, tiled=True
    )

    gradients = pl.pallas_call(
        attend_kernel,
        in_specs=[smem, smem, vmem, vmem, vmem],
        out_specs=vmem,
        out_shape=jax.ShapeDtypeStruct((128, BACK_ROWS, 128), BF16),
        scratch_shapes=[
            pltpu.VMEM((3, BLOCK, BLOCK), BF16),
            pltpu.VMEM((3, BLOCK, BLOCK), BF16),
            pltpu.VMEM((2048, 128), F32),
            pltpu.VMEM((WIDTH, 2 * BLOCK, D), BF16),
            pltpu.VMEM((WIDTH, 2 * BLOCK, D), BF16),
            pltpu.VMEM((3 * BLOCK, D), BF16),
            pltpu.VMEM((3 * BLOCK, D), BF16),
            pltpu.VMEM((D, 3 * BLOCK), BF16),
            pltpu.VMEM((12, 128, 128), F32),
            pltpu.VMEM((5, WIDTH, 128, 128), F32),
            pltpu.VMEM((5, WIDTH, 128, 128), F32),
            pltpu.VMEM((D, WIDTH * 128), F32),
            pltpu.VMEM((WIDTH, D, 2 * BLOCK), BF16),
            pltpu.VMEM((3 * BLOCK, D), F32),
            pltpu.VMEM((3 * BLOCK, D), F32),
        ],
        compiler_params=params,
        name="attend",
    )(me, segment, place2, doc2, arrived)

    back = lax.all_to_all(gradients, ("ctx", "head"), split_axis=0, concat_axis=0, tiled=True)

    return pl.pallas_call(
        return_kernel,
        grid=(GROUPS,),
        in_specs=[
            smem,
            whole,
            pl.BlockSpec((PAIRS, 1, BACK_ROWS, 128), lambda g: (0, g, 0, 0)),
        ],
        out_specs=[
            pl.BlockSpec((128, WIDTH * D), lambda g: (0, g)),
            pl.BlockSpec((128, D), lambda g: (0, g)),
            pl.BlockSpec((128, D), lambda g: (0, g)),
        ],
        out_shape=[
            jax.ShapeDtypeStruct((128, GROUPS * WIDTH * D), BF16),
            jax.ShapeDtypeStruct((128, GROUPS * D), BF16),
            jax.ShapeDtypeStruct((128, GROUPS * D), BF16),
        ],
        scratch_shapes=[
            pltpu.VMEM((512, 512), BF16),
            pltpu.VMEM((128, 384), BF16),
            pltpu.VMEM((128, 384), BF16),
        ],
        compiler_params=params,
        name="to_rows",
    )(me, place2, back.reshape(PAIRS, GROUPS, BACK_ROWS, 128))


def solution(mesh):
    spec = P(("ctx", "head"), None)
    in_specs = (spec, spec, spec, spec, P(("ctx", "head")), P(), P())
    return jax.shard_map(
        shards, mesh=mesh, in_specs=in_specs, out_specs=(spec, spec, spec), check_vma=False
    )
```

time: 633 us -> 174 us (0.27); the launches traced: 622 us -> 173 us
  local copies, waits for them, and re-layouts: 259 us -> 0 us
  waiting for transfers between devices: 129 us -> 0 us
  blocking collectives: 0 us -> 121 us
  matrix products: 99.2 us -> 0 us
  starting transfers between devices: 96.7 us -> 0 us
  Pallas kernels: 0 us -> 51.1 us
  other arithmetic: 36.3 us -> 0 us
    all_to_all x0 -> x2, blocking collectives: none -> 121 us  [the longest x1 73.6 us: shards(): lax.all_to_all(sent.reshape(128, SEND_ROWS, 128), ('ctx', 'head'), split_...]
    all_to_all x14 -> x0, waiting for transfers between devices: 111 us -> none  [the longest x1 28.9 us: shards(): lax.all_to_all(to_sources(grad_query_rows), 'ctx', split_axis=0, concat_a...]
    dot_general x28 -> x0, matrix products: 99.2 us -> none  [the longest x4 27.6 us: step(): jnp.einsum('kgqs,ksd->kgqd', score_gradient, keys_here, preferred_element...]
    all_to_all x14 -> x0, starting transfers between devices: 88.1 us -> none  [the longest x1 11.3 us: shards(): lax.all_to_all(to_slots(key), 'ctx', split_axis=0, concat_axis=0, tiled=T...]
    scatter x3 -> x0, local copies, waits for them, and re-layouts: 64.1 us -> none  [the longest x1 60.3 us: shards(): jnp.zeros((every_token,), jnp.int32).at[place]]
    all_to_all x14 -> x0, local copies, waits for them, and re-layouts: 61.5 us -> none  [the longest x1 13.3 us: shards(): lax.all_to_all(to_slots(weighted), 'ctx', split_axis=0, concat_axis=0, ti...]
    gather x18 -> x0, local copies, waits for them, and re-layouts: 53.5 us -> none  [the longest x4 11.9 us: to_slots(): return rows[send_order].reshape(ctx_count, sent, rows.shape[1])]
    pallas_call x0 -> x3, Pallas kernels: none -> 51.1 us  [the longest x1 34.5 us: shards(): pl.pallas_call(attend_kernel, in_specs=[smem, smem, vmem, vmem, vmem], ou...]
  transfers between devices with their start and end apart: 17 -> 0, of which waited for: 13 -> 0; matrix products, arithmetic and copies ran while one was open for 33% -> 0% of each run, Pallas kernels for 0% -> 0%
where the time goes in v1:
time: 174 us; the launch traced here: 173 us
  blocking collectives  121 us (70%)
  Pallas kernels  51.1 us (29%)
    all_to_all x1, blocking collectives, shards(): lax.all_to_all(sent.reshape(128, SEND_ROWS, 128), ('ctx', 'head'), split_...  73.6 us
    all_to_all x1, blocking collectives, shards(): lax.all_to_all(gradients, ('ctx', 'head'), split_axis=0, concat_axis=0, t...  47.8 us
    pallas_call x1, Pallas kernels, shards(): pl.pallas_call(attend_kernel, in_specs=[smem, smem, vmem, vmem, vmem], ou...  34.5 us
    pallas_call x1, Pallas kernels, shards(): pl.pallas_call(send_kernel, grid=(GROUPS,), in_specs=[smem, whole, pl.Blo...  9.08 us
    pallas_call x1, Pallas kernels, shards(): pl.pallas_call(return_kernel, grid=(GROUPS,), in_specs=[smem, whole, pl.B...  7.49 us

profile of v1, /device:TPU:1, one launch (start us, length us, event | category | flops | bytes accessed | tf_op | source)
XLA Modules:
  0.0 173.1 jit_solution(11933381193968821385)
XLA Ops:
  0.6 9.1 %to_blocks.1 = bf16[16,8,152,128]{3,2,1,0:T(8,128)(2,1)} custom-call(s32[1]{0:T(128)} %bitcast.me_ref, s32[128,128]{1,0:T(8,128)} %bitcast.8, f32[1,128]{1,0:T(1,128)} %bitcast.12, bf16[128,8192]{1,0:T(8,128)(2,1)} %q_ref.1, bf16[128,1024]{1,0:T(8,128)(2,1)} %k_ref.1, bf16[128,1024]{1,0:T(8,128)(2,1)} %v_ref.1, bf16[128,8192]{1,0:T(8,128)(2,1)} %g_ref.1), custom_call_target="tpu_custom_call" | custom-call | tf_op jit(solution)/shard_map/to_blocks/pallas_call | solution.py:306
  9.7 73.6 %all_to_all.10.in_ref = bf16[128,152,128]{2,1,0:T(8,128)(2,1)} all-to-all(bf16[128,152,128]{2,1,0:T(8,128)(2,1)} %bitcast.6), channel_id=1, replica_groups=mesh['ctx'=32,'head'=4] {'ctx','head'}, dimensions={0} | all-to-all | bytes 9961472 | tf_op jit(solution)/shard_map/all_to_all | solution.py:331
  83.3 34.5 %attend.1 = bf16[128,88,128]{2,1,0:T(8,128)(2,1)} custom-call(s32[1]{0:T(128)} %bitcast.me_ref, s32[16384]{0:T(1024)} %seg_ref.1, s32[128,128]{1,0:T(8,128)} %bitcast.9, s32[128,128]{1,0:T(8,128)} %bitcast.11, bf16[128,152,128]{2,1,0:T(8,128)(2,1)} %all_to_all.10.in_ref), custom_call_target="tpu_custom_call" | custom-call | tf_op jit(solution)/shard_map/attend/pallas_call | solution.py:335
  117.8 47.8 %all_to_all.11 = bf16[128,88,128]{2,1,0:T(8,128)(2,1)} all-to-all(bf16[128,88,128]{2,1,0:T(8,128)(2,1)} %attend.1), channel_id=1, replica_groups=mesh['ctx'=32,'head'=4] {'ctx','head'}, dimensions={0} | all-to-all | bytes 5767168 | tf_op jit(solution)/shard_map/all_to_all | solution.py:361
  165.6 7.5 %to_rows.1 = (bf16[128,8192]{1,0:T(8,128)(2,1)}, bf16[128,1024]{1,0:T(8,128)(2,1)}, bf16[128,1024]{1,0:T(8,128)(2,1)}) custom-call(s32[1]{0:T(128)} %bitcast.me_ref, s32[128,128]{1,0:T(8,128)} %bitcast.10, bf16[16,8,88,128]{3,2,1,0:T(8,128)(2,1)} %bitcast.7), custom_call_target="tpu_custom_call" | custom-call | tf_op jit(solution)/shard_map/to_rows/pallas_call | solution.py:363

commit v2 on v1

v2 whole, which is shorter than its diff:
```python
import functools

import jax
import jax.numpy as jnp
from jax import lax
from jax.experimental import pallas as pl
from jax.experimental.pallas import tpu as pltpu
from jax.sharding import PartitionSpec as P

GROUPS = 8
WIDTH = 8
D = 128
BLOCK = 512
PAIRS = 16
SPAN = 3 * BLOCK
SCALE = D ** (-0.5)
LOG2E = 1.4426950408889634
NEG = -1e30
F32 = jnp.float32
BF16 = jnp.bfloat16

SEND_ROWS = 8 * (2 * WIDTH + 3)
BACK_ROWS = 8 * (WIDTH + 3)
VMEM_LIMIT = 56 * 1024 * 1024
PER = 8
QB = 1
IN_ORDER = (4, 0, 1, 2, 3)


def iota(shape, dim):
    return lax.broadcasted_iota(jnp.int32, shape, dim)


def dot(a, b):
    return jnp.dot(a, b, preferred_element_type=F32)


def dot_nt(a, b):
    return lax.dot_general(a, b, (((1,), (1,)), ((), ())), preferred_element_type=F32)


def onehot(index, code):
    return (index == code).astype(F32).astype(BF16)


def token_codes(place_ref, me):
    row = place_ref[pl.ds(me, 1), :]
    dest = lax.shift_right_logical(row, 9)
    across = jnp.broadcast_to(dest.astype(F32), (128, 128))
    before = (across == jnp.transpose(across)) & (iota((128, 128), 0) < iota((128, 128), 1))
    rank = jnp.sum(before.astype(F32), axis=0, keepdims=True).astype(jnp.int32)
    pair, half, odd = lax.shift_right_logical(dest, 1), dest & 1, me & 1
    own = pair * 8 + (half ^ odd) * 4 + rank
    later = (half == 1) & (pair < PAIRS - 1)
    halo_key = jnp.where(later, pair * 8 + 8 + odd * 4 + rank, -1)
    halo_value = jnp.where(later, pair * 8 + 8 + (1 - odd) * 4 + rank, -1)
    return own, halo_key, halo_value


def tiles_to(out_ref, start, tiles):
    n = out_ref.shape[0]
    for i in range(0, len(tiles), 2):
        part = [t.reshape(n, 8, 128) for t in tiles[i : i + 2]]
        part = jnp.concatenate(part, axis=1) if len(part) == 2 else part[0]
        at = start + 8 * i
        out_ref[:, at : at + part.shape[1], :] = part.astype(BF16)


def send_kernel(me_ref, place_ref, adv_ref, q_ref, g_ref, k_ref, v_ref, out_ref, own, halo_k, halo_v, adv):
    @pl.when(pl.program_id(0) == 0)
    def _():
        for ref, code in zip((own, halo_k, halo_v), token_codes(place_ref, me_ref[0])):
            ref[...] = onehot(iota((128, 128), 0), code)
        adv[...] = jnp.transpose(jnp.broadcast_to(adv_ref[...], (128, 128)))

    weight, move = adv[...], own[...]
    grad = jnp.concatenate(
        [(g_ref[:, h * D : (h + 1) * D].astype(F32) * weight).astype(BF16) for h in range(WIDTH)], axis=1
    )
    tiles = []
    for block in (q_ref[...], grad):
        moved = dot(move, block)
        tiles += [moved[:, h * D : (h + 1) * D] for h in range(WIDTH)]
    tiles += [dot(move, k_ref[...]), dot(move, v_ref[...])]
    tiles += [dot(halo_k[...], k_ref[...]) + dot(halo_v[...], v_ref[...])]
    tiles_to(out_ref.at[:, 0], 0, tiles)


def source_maps(place, block, spread_ref, gather_ref, column):
    own = lax.shift_right_logical(place, 9) == block
    member = own.astype(F32)
    earlier = onehot(jnp.int32(1), (iota((128, 128), 0) < iota((128, 128), 1)).astype(jnp.int32))
    rank = dot(member.astype(BF16), earlier)
    picked = jnp.where(own, (place - block * BLOCK + 1).astype(F32), 0.0)
    for r in range(4):
        part = jnp.sum(jnp.where(rank == r, picked, 0.0), axis=1, keepdims=True) - 1.0
        column[pl.ds(r, 128, stride=4), :] = jnp.broadcast_to(part, (128, 128))
    for b in range(4):
        at = slice(b * 128, (b + 1) * 128)
        whole = column[at, :]
        gather_ref[at, :] = jnp.concatenate(
            [onehot(iota((128, 128), 1) + 128 * c, whole.astype(jnp.int32)) for c in range(4)], axis=1
        )
        row = jnp.transpose(whole)[0:1, :].astype(jnp.int32)
        spread_ref[:, at] = onehot(iota((BLOCK, 128), 0), row)


def attend_kernel(
    me_ref, place_ref, doc_ref, in_hbm, out_hbm,
    in_ref, out_ref, to_pos, to_src, column, arrived, qs, ws, ks, vs, kt, doc_t, dq_t, dk_acc, dv_acc, counts,
    in_sem, out_sem,
):
    def copy_in(i):
        at = pl.ds(32 * i, 32 if i < 4 else 24)
        return pltpu.make_async_copy(in_hbm.at[:, at], in_ref.at[:, at], in_sem.at[i])

    for i in IN_ORDER:
        copy_in(i).start()

    pair = lax.shift_right_logical(me_ref[0], 3)
    place = place_ref[...]
    even = (iota((128, 128), 0) & 1) == 0
    place_f = place.astype(F32)
    swapped = jnp.where(even, pltpu.roll(place_f, 127, 0), pltpu.roll(place_f, 1, 0)).astype(jnp.int32)
    for i, (rows, block) in enumerate(
        ((place, 2 * pair), (swapped, 2 * pair + 1), (place, 2 * pair - 1), (swapped, 2 * pair - 1))
    ):
        source_maps(rows, block, to_pos.at[i], to_src.at[i], column.at[i])

    docs = doc_ref[...]
    block_at = iota((128, 128), 0)
    last = iota((128, 128), 1) == 127
    for ib in range(8):
        block = 8 * pair + ib
        first_doc = doc_ref[pl.ds(block, 1), :][:, 0:1]
        near = last & (block_at < block) & (block_at >= block - 4) & (docs >= first_doc)
        counts[ib] = 1 + jnp.sum(near.astype(F32)).astype(jnp.int32)
    for b in range(12):
        at = 8 * pair - 4 + b
        doc = doc_ref[pl.ds(jnp.maximum(at, 0), 1), :].astype(F32)
        doc = jnp.where(at >= 0, doc, -2.0)
        doc_t[b * 128 : (b + 1) * 128, :] = jnp.transpose(jnp.broadcast_to(doc, (128, 128)))
    dk_acc[...] = jnp.zeros_like(dk_acc)
    dv_acc[...] = jnp.zeros_like(dv_acc)

    upper = iota((64, 8, 128), 1) < 4

    def halves(tile):
        rows = in_ref[:, 8 * tile : 8 * tile + 8, :].astype(F32).reshape(64, 16, 128)
        a, b = rows[:, :8], rows[:, 8:]
        return (
            jnp.where(upper, a, b).reshape(BLOCK, 128).astype(BF16),
            jnp.where(upper, b, a).reshape(BLOCK, 128).astype(BF16),
        )

    def placed(t, count, half, map_at):
        both = jnp.concatenate([arrived[t + i, half] for i in range(count)], axis=1)
        return dot(to_pos[map_at], both).astype(BF16)

    for i in IN_ORDER:
        copy_in(i).wait()
        tiles = range(4 * i, min(4 * i + 4, 19))
        for t in tiles:
            arrived[t, 0], arrived[t, 1] = halves(t)
        if i < 4:
            target, first = (qs, 4 * i) if i < 2 else (ws, 4 * i - 8)
            for h in range(0, 4, 2):
                for b in range(2):
                    moved = placed(4 * i + h, 2, b, b)
                    at = slice(b * BLOCK, (b + 1) * BLOCK)
                    target[first + h, at, :] = moved[:, :128]
                    target[first + h + 1, at, :] = moved[:, 128:]
        else:
            for b in range(2):
                moved = placed(16, 2, b, b)
                at = slice((b + 1) * BLOCK, (b + 2) * BLOCK)
                ks[at, :] = moved[:, :128]
                vs[at, :] = moved[:, 128:]
            ks[:BLOCK, :] = placed(18, 1, 0, 2)
            vs[:BLOCK, :] = placed(18, 1, 1, 3)
            kt[...] = dot_nt(onehot(iota((128, 128), 0), iota((128, 128), 1)), ks[...]).astype(BF16)

    def over(first, n):
        length = n * 128
        for ib in [first + k for k in range(QB)]:
            rows = pl.ds(pl.multiple_of(ib * 128, 128), 128)
            query_doc = doc_ref[pl.ds(8 * pair + ib, 1), :].astype(F32)
            window = pl.ds(pl.multiple_of((ib + 5 - n) * 128, 128), length)
            keys, values, keys_t = ks[window, :], vs[window, :], kt[:, window]
            later = iota((length, 128), 0) - iota((length, 128), 1) > length - 128
            bias = jnp.where((doc_t[window, :] == query_doc) & ~later, 0.0, NEG)
            bias = jnp.concatenate([bias] * PER, axis=1)
            all_weights, all_dscore, all_query, all_grad = [], [], [], []
            for h in range(0, WIDTH, PER):
                query = jnp.concatenate([qs[h + k, rows, :] for k in range(PER)], axis=0)
                grad = jnp.concatenate([ws[h + k, rows, :] for k in range(PER)], axis=0)
                score = dot_nt(keys, query) * (SCALE * LOG2E) + bias
                prob = jnp.exp2(score - jnp.max(score, axis=0, keepdims=True))
                prob = prob * (1.0 / jnp.sum(prob, axis=0, keepdims=True))
                weights = prob.astype(BF16)
                dprob = dot_nt(values, grad)
                delta = jnp.sum(weights.astype(F32) * dprob, axis=0, keepdims=True)
                dscore = (prob * SCALE * (dprob - delta)).astype(BF16)
                dq = dot(keys_t, dscore).astype(BF16)
                for k in range(PER):
                    dq_t[h + k, :, rows] = dq[:, k * 128 : (k + 1) * 128]
                all_weights.append(weights)
                all_dscore.append(dscore)
                all_query.append(query)
                all_grad.append(grad)
            dv_acc[window, :] += dot(
                jnp.concatenate(all_weights, axis=1), jnp.concatenate(all_grad, axis=0)
            )
            dk_acc[window, :] += dot(
                jnp.concatenate(all_dscore, axis=1), jnp.concatenate(all_query, axis=0)
            )

    def query_blocks(i, carry):
        first = i * QB
        count = counts[first]
        for k in range(1, QB):
            count = jnp.maximum(count, counts[first + k])
        pl.when(count <= 2)(lambda: over(first, 2))
        pl.when(count == 3)(lambda: over(first, 3))
        pl.when(count >= 4)(lambda: over(first, 5))
        return carry

    lax.fori_loop(0, 8 // QB, query_blocks, 0)

    def woven(one, two):
        a, b = one.reshape(64, 8, 128), two.reshape(64, 8, 128)
        rows = jnp.concatenate([jnp.where(upper, a, b), jnp.where(upper, b, a)], axis=1)
        return rows.reshape(1024, 128)

    def copy_out(i):
        at = pl.ds(16 * i, 16 if i < 4 else 24)
        return pltpu.make_async_copy(out_ref.at[:, at], out_hbm.at[:, at], out_sem.at[i])

    def rounded(b):
        at = slice(b * BLOCK, (b + 1) * BLOCK)
        return dk_acc[at, :].astype(BF16), dv_acc[at, :].astype(BF16)

    both = [dot(to_src[b], jnp.concatenate(rounded(b + 1), axis=1)) for b in range(2)]
    halo_key, halo_value = rounded(0)
    tiles = [woven(both[0][:, i * 128 : (i + 1) * 128], both[1][:, i * 128 : (i + 1) * 128]) for i in range(2)]
    tiles.append(woven(dot(to_src[2], halo_key), dot(to_src[3], halo_value)))
    tiles_to(out_ref, 8 * WIDTH, tiles)
    copy_out(4).start()
    for h in range(0, WIDTH, 2):
        both = [
            dot_nt(
                to_src[b],
                jnp.concatenate([dq_t[h + i, :, b * BLOCK : (b + 1) * BLOCK] for i in range(2)], axis=0),
            )
            for b in range(2)
        ]
        tiles = [woven(both[0][:, i * 128 : (i + 1) * 128], both[1][:, i * 128 : (i + 1) * 128]) for i in range(2)]
        tiles_to(out_ref, 8 * h, tiles)
        copy_out(h // 2).start()
    for i in range(5):
        copy_out(i).wait()


def return_kernel(me_ref, place_ref, in_ref, dq_ref, dk_ref, dv_ref, own, keys, values):
    @pl.when(pl.program_id(0) == 0)
    def _():
        def column(code):
            return jnp.transpose(jnp.broadcast_to(code.astype(F32), (128, 128))).astype(jnp.int32)

        def wide(code, tile):
            spread = lax.shift_right_logical(code, 3) * 16 + (code & 7) + 8 * tile
            return jnp.where(code >= 0, spread, -1)

        own_c, key_c, value_c = [column(c) for c in token_codes(place_ref, me_ref[0])]
        for at in range(2):
            lanes = iota((128, 128), 1) + 128 * at
            cols = slice(at * 128, (at + 1) * 128)
            for i in range(2):
                own[i * 128 : (i + 1) * 128, cols] = onehot(lanes, wide(own_c, i))
        keys[...] = onehot(iota((128, 128), 1), key_c)
        values[...] = onehot(iota((128, 128), 1), value_c)

    def pair_of(tile):
        return in_ref[:, 0, 8 * tile : 8 * tile + 16, :].reshape(256, 128)

    both = own[...]
    for h in range(0, WIDTH, 4):
        moved = dot(both, jnp.concatenate([pair_of(h), pair_of(h + 2)], axis=1)).astype(BF16)
        for i, (a, b) in enumerate(((0, 0), (1, 0), (0, 1), (1, 1))):
            dq_ref[:, (h + i) * D : (h + i + 1) * D] = moved[a * 128 : (a + 1) * 128, b * 128 : (b + 1) * 128]
    moved = dot(both, pair_of(WIDTH))
    halo = in_ref[:, 0, 8 * WIDTH + 16 :, :].astype(F32).reshape(128, 128).astype(BF16)
    dk_ref[...] = (moved[:128] + dot(keys[...], halo)).astype(BF16)
    dv_ref[...] = (moved[128:] + dot(values[...], halo)).astype(BF16)


SMEM = pl.BlockSpec(memory_space=pltpu.SMEM)
VMEM = pl.BlockSpec(memory_space=pltpu.VMEM)
ANY = pl.BlockSpec(memory_space=pl.ANY)
WHOLE = pl.BlockSpec((128, 128), lambda g: (0, 0))


def params():
    return pltpu.CompilerParams(vmem_limit_bytes=VMEM_LIMIT)


def exchanged(rows):
    return lax.all_to_all(rows, ("ctx", "head"), split_axis=0, concat_axis=0, tiled=True)


def sent(me, place2, advantage, query, grad_out, key, value):
    wide = pl.BlockSpec((128, WIDTH * D), lambda g: (0, g))
    narrow = pl.BlockSpec((128, D), lambda g: (0, g))
    square = pltpu.VMEM((128, 128), BF16)
    out = pl.pallas_call(
        send_kernel,
        grid=(GROUPS,),
        in_specs=[SMEM, WHOLE, pl.BlockSpec((1, 128), lambda g: (0, 0)), wide, wide, narrow, narrow],
        out_specs=pl.BlockSpec((PAIRS, 1, SEND_ROWS, 128), lambda g: (0, g, 0, 0)),
        out_shape=jax.ShapeDtypeStruct((PAIRS, GROUPS, SEND_ROWS, 128), BF16),
        scratch_shapes=[square, square, square, pltpu.VMEM((128, 128), F32)],
        compiler_params=params(),
        name="to_blocks",
    )(me, place2, advantage.reshape(1, 128), query, grad_out, key, value)
    return out.reshape(PAIRS * GROUPS, SEND_ROWS, 128)


def shards(query, key, value, grad_out, advantage, place, segment):
    me = (lax.axis_index("ctx") * 4 + lax.axis_index("head")).astype(jnp.int32).reshape(1)
    place2 = place.reshape(128, 128)
    doc2 = segment.reshape(128, 128)
    arrived = exchanged(sent(me, place2, advantage, query, grad_out, key, value))

    maps = pltpu.VMEM((4, BLOCK, BLOCK), BF16)
    heads = pltpu.VMEM((WIDTH, 2 * BLOCK, D), BF16)
    gradients = pl.pallas_call(
        attend_kernel,
        in_specs=[SMEM, VMEM, VMEM, ANY],
        out_specs=ANY,
        out_shape=jax.ShapeDtypeStruct((128, BACK_ROWS, 128), BF16),
        scratch_shapes=[
            pltpu.VMEM((128, SEND_ROWS, 128), BF16),
            pltpu.VMEM((128, BACK_ROWS, 128), BF16),
            maps,
            maps,
            pltpu.VMEM((4, BLOCK, 128), F32),
            pltpu.VMEM((19, 2, BLOCK, 128), BF16),
            heads,
            heads,
            pltpu.VMEM((SPAN, D), BF16),
            pltpu.VMEM((SPAN, D), BF16),
            pltpu.VMEM((D, SPAN), BF16),
            pltpu.VMEM((SPAN, 128), F32),
            pltpu.VMEM((WIDTH, D, 2 * BLOCK), BF16),
            pltpu.VMEM((SPAN, D), F32),
            pltpu.VMEM((SPAN, D), F32),
            pltpu.SMEM((8,), jnp.int32),
            pltpu.SemaphoreType.DMA((5,)),
            pltpu.SemaphoreType.DMA((5,)),
        ],
        compiler_params=params(),
        name="attend",
    )(me, place2, doc2, arrived)

    back = exchanged(gradients)
    rows = BACK_ROWS
    return pl.pallas_call(
        return_kernel,
        grid=(GROUPS,),
        in_specs=[SMEM, WHOLE, pl.BlockSpec((PAIRS, 1, rows, 128), lambda g: (0, g, 0, 0))],
        out_specs=[
            pl.BlockSpec((128, WIDTH * D), lambda g: (0, g)),
            pl.BlockSpec((128, D), lambda g: (0, g)),
            pl.BlockSpec((128, D), lambda g: (0, g)),
        ],
        out_shape=[
            jax.ShapeDtypeStruct((128, GROUPS * WIDTH * D), BF16),
            jax.ShapeDtypeStruct((128, GROUPS * D), BF16),
            jax.ShapeDtypeStruct((128, GROUPS * D), BF16),
        ],
        scratch_shapes=[
            pltpu.VMEM((256, 256), BF16),
            pltpu.VMEM((128, 128), BF16),
            pltpu.VMEM((128, 128), BF16),
        ],
        compiler_params=params(),
        name="to_rows",
    )(me, place2, back.reshape(PAIRS, GROUPS, rows, 128))


def solution(mesh):
    spec = P(("ctx", "head"), None)
    in_specs = (spec, spec, spec, spec, P(("ctx", "head")), P(), P())
    return jax.shard_map(
        shards, mesh=mesh, in_specs=in_specs, out_specs=(spec, spec, spec), check_vma=False
    )
```

time: 174 us -> 159 us (0.914)
  Pallas kernels: 51.1 us -> 37.9 us
    pallas_call x3, Pallas kernels: 51.1 us -> 37.9 us  [the longest x1 23 us: shards(): pl.pallas_call(attend_kernel, in_specs=[SMEM, VMEM, VMEM, ANY], out_specs...]
where the time goes in v2:
time: 159 us
  blocking collectives  121 us (76%)
  Pallas kernels  37.9 us (24%)
    all_to_all x2, blocking collectives, exchanged(): lax.all_to_all(rows, ('ctx', 'head'), split_axis=0, concat_axis=0, tiled=...  121 us
    pallas_call x1, Pallas kernels, shards(): pl.pallas_call(attend_kernel, in_specs=[SMEM, VMEM, VMEM, ANY], out_specs...  23 us
    pallas_call x1, Pallas kernels, sent(): pl.pallas_call(send_kernel, grid=(GROUPS,), in_specs=[SMEM, WHOLE, pl.Blo...  8.05 us
    pallas_call x1, Pallas kernels, shards(): pl.pallas_call(return_kernel, grid=(GROUPS,), in_specs=[SMEM, WHOLE, pl.B...  6.89 us

profile of v2, /device:TPU:1, one launch (start us, length us, event | category | flops | bytes accessed | tf_op | source)
XLA Modules:
  0.0 159.1 jit_solution(11507535263134050831)
XLA Ops:
  0.6 8.0 %to_blocks.1 = bf16[16,8,152,128]{3,2,1,0:T(8,128)(2,1)} custom-call(s32[1]{0:T(128)} %bitcast.me_ref, s32[128,128]{1,0:T(8,128)} %bitcast.8, f32[1,128]{1,0:T(1,128)} %bitcast.12, bf16[128,8192]{1,0:T(8,128)(2,1)} %q_ref.1, bf16[128,8192]{1,0:T(8,128)(2,1)} %g_ref.1, bf16[128,1024]{1,0:T(8,128)(2,1)} %k_ref.1, bf16[128,1024]{1,0:T(8,128)(2,1)} %v_ref.1), custom_call_target="tpu_custom_call" | custom-call | tf_op jit(solution)/shard_map/to_blocks/pallas_call | solution.py:315
  8.7 73.6 %all_to_all.10.in_hbm = bf16[128,152,128]{2,1,0:T(8,128)(2,1)} all-to-all(bf16[128,152,128]{2,1,0:T(8,128)(2,1)} %bitcast.6), channel_id=1, replica_groups=mesh['ctx'=32,'head'=4] {'ctx','head'}, dimensions={0} | all-to-all | bytes 9961472 | tf_op jit(solution)/shard_map/all_to_all | solution.py:308
  82.3 23.0 %attend.1 = bf16[128,88,128]{2,1,0:T(8,128)(2,1)} custom-call(s32[1]{0:T(128)} %bitcast.me_ref, s32[128,128]{1,0:T(8,128)} %bitcast.9, s32[128,128]{1,0:T(8,128)} %bitcast.11, bf16[128,152,128]{2,1,0:T(8,128)(2,1)} %all_to_all.10.in_hbm), custom_call_target="tpu_custom_call" | custom-call | tf_op jit(solution)/shard_map/attend/pallas_call | solution.py:336
  105.3 47.0 %all_to_all.11 = bf16[128,88,128]{2,1,0:T(8,128)(2,1)} all-to-all(bf16[128,88,128]{2,1,0:T(8,128)(2,1)} %attend.1), channel_id=1, replica_groups=mesh['ctx'=32,'head'=4] {'ctx','head'}, dimensions={0} | all-to-all | bytes 5767168 | tf_op jit(solution)/shard_map/all_to_all | solution.py:308
  152.3 6.9 %to_rows.1 = (bf16[128,8192]{1,0:T(8,128)(2,1)}, bf16[128,1024]{1,0:T(8,128)(2,1)}, bf16[128,1024]{1,0:T(8,128)(2,1)}) custom-call(s32[1]{0:T(128)} %bitcast.me_ref, s32[128,128]{1,0:T(8,128)} %bitcast.10, bf16[16,8,88,128]{3,2,1,0:T(8,128)(2,1)} %bitcast.7), custom_call_target="tpu_custom_call" | custom-call | tf_op jit(solution)/shard_map/to_rows/pallas_call | solution.py:367

commit v3 on v2

--- a/solution.py
+++ b/solution.py
@@ -1,5 +1,3 @@
-import functools
-
 import jax
 import jax.numpy as jnp
 from jax import lax
@@ -44,7 +42,7 @@
 
 
 def token_codes(place_ref, me):
-    row = place_ref[pl.ds(me, 1), :]
+    row = place_ref[pl.ds(me & 7, 1), :]
     dest = lax.shift_right_logical(row, 9)
     across = jnp.broadcast_to(dest.astype(F32), (128, 128))
     before = (across == jnp.transpose(across)) & (iota((128, 128), 0) < iota((128, 128), 1))
@@ -66,24 +64,58 @@
         out_ref[:, at : at + part.shape[1], :] = part.astype(BF16)
 
 
-def send_kernel(me_ref, place_ref, adv_ref, q_ref, g_ref, k_ref, v_ref, out_ref, own, halo_k, halo_v, adv):
-    @pl.when(pl.program_id(0) == 0)
-    def _():
-        for ref, code in zip((own, halo_k, halo_v), token_codes(place_ref, me_ref[0])):
-            ref[...] = onehot(iota((128, 128), 0), code)
-        adv[...] = jnp.transpose(jnp.broadcast_to(adv_ref[...], (128, 128)))
-
-    weight, move = adv[...], own[...]
-    grad = jnp.concatenate(
-        [(g_ref[:, h * D : (h + 1) * D].astype(F32) * weight).astype(BF16) for h in range(WIDTH)], axis=1
-    )
-    tiles = []
-    for block in (q_ref[...], grad):
-        moved = dot(move, block)
-        tiles += [moved[:, h * D : (h + 1) * D] for h in range(WIDTH)]
-    tiles += [dot(move, k_ref[...]), dot(move, v_ref[...])]
-    tiles += [dot(halo_k[...], k_ref[...]) + dot(halo_v[...], v_ref[...])]
-    tiles_to(out_ref.at[:, 0], 0, tiles)
+def fetch_place(place_hbm, place_ref, me, sem):
+    first = pl.multiple_of(lax.shift_right_logical(me, 3) * 8, 8)
+    copy = pltpu.make_async_copy(place_hbm.at[pl.ds(first, 8), :], place_ref, sem)
+    copy.start()
+    return copy
+
+
+def send_kernel(
+    me_ref, place_hbm, adv_hbm, q_hbm, g_hbm, k_hbm, v_hbm, out_hbm,
+    place_ref, adv_ref, q_ref, g_ref, k_ref, v_ref, out_ref, sems, small,
+):
+    place_copy = fetch_place(place_hbm, place_ref, me_ref[0], small.at[0])
+    adv_copy = pltpu.make_async_copy(adv_hbm, adv_ref, small.at[1])
+    adv_copy.start()
+    pairs = ((q_hbm, q_ref), (g_hbm, g_ref), (k_hbm, k_ref), (v_hbm, v_ref))
+
+    def copies_in(g):
+        for i, (source, into) in enumerate(pairs):
+            width = WIDTH * D if i < 2 else D
+            at = slice(g * width, (g + 1) * width)
+            yield pltpu.make_async_copy(source.at[:, at], into.at[:, at], sems.at[i, g])
+
+    def copy_out(g):
+        return pltpu.make_async_copy(out_ref.at[:, g], out_hbm.at[:, g], sems.at[4, g])
+
+    for g in range(GROUPS):
+        for copy in copies_in(g):
+            copy.start()
+    place_copy.wait()
+    adv_copy.wait()
+    rows = iota((128, 128), 0)
+    own, halo_k, halo_v = [onehot(rows, code) for code in token_codes(place_ref, me_ref[0])]
+    weight = jnp.transpose(jnp.broadcast_to(adv_ref[...], (128, 128)))
+    for g in range(GROUPS):
+        for copy in copies_in(g):
+            copy.wait()
+        wide = slice(g * WIDTH * D, (g + 1) * WIDTH * D)
+        narrow = slice(g * D, (g + 1) * D)
+        grad = g_ref[:, wide]
+        grad = jnp.concatenate(
+            [(grad[:, h * D : (h + 1) * D].astype(F32) * weight).astype(BF16) for h in range(WIDTH)], axis=1
+        )
+        tiles = []
+        for block in (q_ref[:, wide], grad):
+            moved = dot(own, block)
+            tiles += [moved[:, h * D : (h + 1) * D] for h in range(WIDTH)]
+        key, value = k_ref[:, narrow], v_ref[:, narrow]
+        tiles += [dot(own, key), dot(own, value), dot(halo_k, key) + dot(halo_v, value)]
+        tiles_to(out_ref.at[:, g], 0, tiles)
+        copy_out(g).start()
+    for g in range(GROUPS):
+        copy_out(g).wait()
 
 
 def source_maps(place, block, spread_ref, gather_ref, column):
@@ -106,16 +138,24 @@
 
 
 def attend_kernel(
-    me_ref, place_ref, doc_ref, in_hbm, out_hbm,
-    in_ref, out_ref, to_pos, to_src, column, arrived, qs, ws, ks, vs, kt, doc_t, dq_t, dk_acc, dv_acc, counts,
-    in_sem, out_sem,
+    me_ref, place_hbm, doc_hbm, in_hbm, out_hbm,
+    place_ref, doc_ref, in_ref, out_ref, to_pos, to_src, column, arrived, qs, ws, ks, vs, kt, doc_t, dq_t, dk_acc, dv_acc, counts,
+    in_sem, out_sem, small,
 ):
     def copy_in(i):
         at = pl.ds(32 * i, 32 if i < 4 else 24)
         return pltpu.make_async_copy(in_hbm.at[:, at], in_ref.at[:, at], in_sem.at[i])
 
+    tables = [
+        pltpu.make_async_copy(place_hbm, place_ref, small.at[0]),
+        pltpu.make_async_copy(doc_hbm, doc_ref, small.at[1]),
+    ]
+    for copy in tables:
+        copy.start()
     for i in IN_ORDER:
         copy_in(i).start()
+    for copy in tables:
+        copy.wait()
 
     pair = lax.shift_right_logical(me_ref[0], 3)
     place = place_ref[...]
@@ -261,43 +301,68 @@
         copy_out(i).wait()
 
 
-def return_kernel(me_ref, place_ref, in_ref, dq_ref, dk_ref, dv_ref, own, keys, values):
-    @pl.when(pl.program_id(0) == 0)
-    def _():
-        def column(code):
-            return jnp.transpose(jnp.broadcast_to(code.astype(F32), (128, 128))).astype(jnp.int32)
-
-        def wide(code, tile):
-            spread = lax.shift_right_logical(code, 3) * 16 + (code & 7) + 8 * tile
-            return jnp.where(code >= 0, spread, -1)
-
-        own_c, key_c, value_c = [column(c) for c in token_codes(place_ref, me_ref[0])]
-        for at in range(2):
-            lanes = iota((128, 128), 1) + 128 * at
-            cols = slice(at * 128, (at + 1) * 128)
-            for i in range(2):
-                own[i * 128 : (i + 1) * 128, cols] = onehot(lanes, wide(own_c, i))
-        keys[...] = onehot(iota((128, 128), 1), key_c)
-        values[...] = onehot(iota((128, 128), 1), value_c)
-
-    def pair_of(tile):
-        return in_ref[:, 0, 8 * tile : 8 * tile + 16, :].reshape(256, 128)
-
-    both = own[...]
-    for h in range(0, WIDTH, 4):
-        moved = dot(both, jnp.concatenate([pair_of(h), pair_of(h + 2)], axis=1)).astype(BF16)
-        for i, (a, b) in enumerate(((0, 0), (1, 0), (0, 1), (1, 1))):
-            dq_ref[:, (h + i) * D : (h + i + 1) * D] = moved[a * 128 : (a + 1) * 128, b * 128 : (b + 1) * 128]
-    moved = dot(both, pair_of(WIDTH))
-    halo = in_ref[:, 0, 8 * WIDTH + 16 :, :].astype(F32).reshape(128, 128).astype(BF16)
-    dk_ref[...] = (moved[:128] + dot(keys[...], halo)).astype(BF16)
-    dv_ref[...] = (moved[128:] + dot(values[...], halo)).astype(BF16)
+def return_kernel(
+    me_ref, place_hbm, in_hbm, dq_hbm, dk_hbm, dv_hbm, place_ref, in_ref, dq_ref, dk_ref, dv_ref, sems, small
+):
+    place_copy = fetch_place(place_hbm, place_ref, me_ref[0], small.at[0])
+
+    def copy_in(g):
+        return pltpu.make_async_copy(in_hbm.at[:, g], in_ref.at[:, g], sems.at[0, g])
+
+    def copy_dq(g):
+        at = slice(g * WIDTH * D, (g + 1) * WIDTH * D)
+        return pltpu.make_async_copy(dq_ref.at[:, at], dq_hbm.at[:, at], sems.at[1, g])
+
+    for g in range(GROUPS):
+        copy_in(g).start()
+    place_copy.wait()
+
+    def column(code):
+        return jnp.transpose(jnp.broadcast_to(code.astype(F32), (128, 128))).astype(jnp.int32)
+
+    def wide(code, tile):
+        return lax.shift_right_logical(code, 3) * 16 + (code & 7) + 8 * tile
+
+    own_c, key_c, value_c = [column(c) for c in token_codes(place_ref, me_ref[0])]
+    own = jnp.concatenate(
+        [
+            jnp.concatenate([onehot(iota((128, 128), 1) + 128 * at, wide(own_c, i)) for at in range(2)], axis=1)
+            for i in range(2)
+        ],
+        axis=0,
+    )
+    keys, values = onehot(iota((128, 128), 1), key_c), onehot(iota((128, 128), 1), value_c)
+    for g in range(GROUPS):
+        copy_in(g).wait()
+
+        def pair_of(tile):
+            return in_ref[:, g, 8 * tile : 8 * tile + 16, :].reshape(256, 128)
+
+        for h in range(0, WIDTH, 4):
+            moved = dot(own, jnp.concatenate([pair_of(h), pair_of(h + 2)], axis=1)).astype(BF16)
+            for i, (a, b) in enumerate(((0, 0), (1, 0), (0, 1), (1, 1))):
+                at = (g * WIDTH + h + i) * D
+                dq_ref[:, at : at + D] = moved[a * 128 : (a + 1) * 128, b * 128 : (b + 1) * 128]
+        moved = dot(own, pair_of(WIDTH))
+        halo = in_ref[:, g, 8 * WIDTH + 16 :, :].astype(F32).reshape(128, 128).astype(BF16)
+        narrow = slice(g * D, (g + 1) * D)
+        dk_ref[:, narrow] = (moved[:128] + dot(keys, halo)).astype(BF16)
+        dv_ref[:, narrow] = (moved[128:] + dot(values, halo)).astype(BF16)
+        copy_dq(g).start()
+    last = [
+        pltpu.make_async_copy(dk_ref, dk_hbm, small.at[1]),
+        pltpu.make_async_copy(dv_ref, dv_hbm, small.at[2]),
+    ]
+    for copy in last:
+        copy.start()
+    for g in range(GROUPS):
+        copy_dq(g).wait()
+    for copy in last:
+        copy.wait()
 
 
 SMEM = pl.BlockSpec(memory_space=pltpu.SMEM)
-VMEM = pl.BlockSpec(memory_space=pltpu.VMEM)
 ANY = pl.BlockSpec(memory_space=pl.ANY)
-WHOLE = pl.BlockSpec((128, 128), lambda g: (0, 0))
 
 
 def params():
@@ -309,16 +374,22 @@
 
 
 def sent(me, place2, advantage, query, grad_out, key, value):
-    wide = pl.BlockSpec((128, WIDTH * D), lambda g: (0, g))
-    narrow = pl.BlockSpec((128, D), lambda g: (0, g))
-    square = pltpu.VMEM((128, 128), BF16)
     out = pl.pallas_call(
         send_kernel,
-        grid=(GROUPS,),
-        in_specs=[SMEM, WHOLE, pl.BlockSpec((1, 128), lambda g: (0, 0)), wide, wide, narrow, narrow],
-        out_specs=pl.BlockSpec((PAIRS, 1, SEND_ROWS, 128), lambda g: (0, g, 0, 0)),
+        in_specs=[SMEM] + [ANY] * 6,
+        out_specs=ANY,
         out_shape=jax.ShapeDtypeStruct((PAIRS, GROUPS, SEND_ROWS, 128), BF16),
-        scratch_shapes=[square, square, square, pltpu.VMEM((128, 128), F32)],
+        scratch_shapes=[
+            pltpu.VMEM((8, 128), jnp.int32),
+            pltpu.VMEM((1, 128), F32),
+            pltpu.VMEM((128, GROUPS * WIDTH * D), BF16),
+            pltpu.VMEM((128, GROUPS * WIDTH * D), BF16),
+            pltpu.VMEM((128, GROUPS * D), BF16),
+            pltpu.VMEM((128, GROUPS * D), BF16),
+            pltpu.VMEM((PAIRS, GROUPS, SEND_ROWS, 128), BF16),
+            pltpu.SemaphoreType.DMA((5, GROUPS)),
+            pltpu.SemaphoreType.DMA((2,)),
+        ],
         compiler_params=params(),
         name="to_blocks",
     )(me, place2, advantage.reshape(1, 128), query, grad_out, key, value)
@@ -335,10 +406,12 @@
     heads = pltpu.VMEM((WIDTH, 2 * BLOCK, D), BF16)
     gradients = pl.pallas_call(
         attend_kernel,
-        in_specs=[SMEM, VMEM, VMEM, ANY],
+        in_specs=[SMEM, ANY, ANY, ANY],
         out_specs=ANY,
         out_shape=jax.ShapeDtypeStruct((128, BACK_ROWS, 128), BF16),
         scratch_shapes=[
+            pltpu.VMEM((128, 128), jnp.int32),
+            pltpu.VMEM((128, 128), jnp.int32),
             pltpu.VMEM((128, SEND_ROWS, 128), BF16),
             pltpu.VMEM((128, BACK_ROWS, 128), BF16),
             maps,
@@ -357,6 +430,7 @@
             pltpu.SMEM((8,), jnp.int32),
             pltpu.SemaphoreType.DMA((5,)),
             pltpu.SemaphoreType.DMA((5,)),
+            pltpu.SemaphoreType.DMA((2,)),
         ],
         compiler_params=params(),
         name="attend",
@@ -364,24 +438,21 @@
 
     back = exchanged(gradients)
     rows = BACK_ROWS
+    wide = (128, GROUPS * WIDTH * D)
+    narrow = (128, GROUPS * D)
     return pl.pallas_call(
         return_kernel,
-        grid=(GROUPS,),
-        in_specs=[SMEM, WHOLE, pl.BlockSpec((PAIRS, 1, rows, 128), lambda g: (0, g, 0, 0))],
-        out_specs=[
-            pl.BlockSpec((128, WIDTH * D), lambda g: (0, g)),
-            pl.BlockSpec((128, D), lambda g: (0, g)),
-            pl.BlockSpec((128, D), lambda g: (0, g)),
-        ],
-        out_shape=[
-            jax.ShapeDtypeStruct((128, GROUPS * WIDTH * D), BF16),
-            jax.ShapeDtypeStruct((128, GROUPS * D), BF16),
-            jax.ShapeDtypeStruct((128, GROUPS * D), BF16),
-        ],
+        in_specs=[SMEM, ANY, ANY],
+        out_specs=[ANY] * 3,
+        out_shape=[jax.ShapeDtypeStruct(x, BF16) for x in (wide, narrow, narrow)],
         scratch_shapes=[
-            pltpu.VMEM((256, 256), BF16),
-            pltpu.VMEM((128, 128), BF16),
-            pltpu.VMEM((128, 128), BF16),
+            pltpu.VMEM((8, 128), jnp.int32),
+            pltpu.VMEM((PAIRS, GROUPS, rows, 128), BF16),
+            pltpu.VMEM(wide, BF16),
+            pltpu.VMEM(narrow, BF16),
+            pltpu.VMEM(narrow, BF16),
+            pltpu.SemaphoreType.DMA((2, GROUPS)),
+            pltpu.SemaphoreType.DMA((3,)),
         ],
         compiler_params=params(),
         name="to_rows",

time: 159 us -> 155 us (0.975)
  Pallas kernels: 37.9 us -> 34.1 us
    pallas_call x3, Pallas kernels: 37.9 us -> 34.1 us  [the longest x1 22.9 us: shards(): pl.pallas_call(attend_kernel, in_specs=[SMEM, ANY, ANY, ANY], out_specs=A...]
where the time goes in v3:
time: 155 us; the launch traced here: 156 us
  blocking collectives  121 us (78%)
  Pallas kernels  34.1 us (22%)
    all_to_all x2, blocking collectives, exchanged(): lax.all_to_all(rows, ('ctx', 'head'), split_axis=0, concat_axis=0, tiled=...  121 us
    pallas_call x1, Pallas kernels, shards(): pl.pallas_call(attend_kernel, in_specs=[SMEM, ANY, ANY, ANY], out_specs=A...  22.9 us
    pallas_call x1, Pallas kernels, sent(): pl.pallas_call(send_kernel, in_specs=[SMEM] + [ANY] * 6, out_specs=ANY, o...  6.13 us
    pallas_call x1, Pallas kernels, shards(): pl.pallas_call(return_kernel, in_specs=[SMEM, ANY, ANY], out_specs=[ANY]...  5.12 us

profile of v3, /device:TPU:1, one launch (start us, length us, event | category | flops | bytes accessed | tf_op | source)
XLA Modules:
  0.0 155.6 jit_solution(8488159152447380387)
XLA Ops:
  0.6 6.1 %to_blocks.1 = bf16[16,8,152,128]{3,2,1,0:T(8,128)(2,1)} custom-call(s32[1]{0:T(128)} %bitcast.me_ref, s32[128,128]{1,0:T(8,128)} %bitcast.8, f32[1,128]{1,0:T(1,128)} %bitcast.12, bf16[128,8192]{1,0:T(8,128)(2,1)} %q_hbm.1, bf16[128,8192]{1,0:T(8,128)(2,1)} %g_hbm.1, bf16[128,1024]{1,0:T(8,128)(2,1)} %k_hbm.1, bf16[128,1024]{1,0:T(8,128)(2,1)} %v_hbm.1), custom_call_target="tpu_custom_call" | custom-call | tf_op jit(solution)/shard_map/to_blocks/pallas_call | solution.py:377
  6.8 73.6 %all_to_all.10.in_hbm = bf16[128,152,128]{2,1,0:T(8,128)(2,1)} all-to-all(bf16[128,152,128]{2,1,0:T(8,128)(2,1)} %bitcast.6), channel_id=1, replica_groups=mesh['ctx'=32,'head'=4] {'ctx','head'}, dimensions={0} | all-to-all | bytes 9961472 | tf_op jit(solution)/shard_map/all_to_all | solution.py:373
  80.4 22.9 %attend.1 = bf16[128,88,128]{2,1,0:T(8,128)(2,1)} custom-call(s32[1]{0:T(128)} %bitcast.me_ref, s32[128,128]{1,0:T(8,128)} %bitcast.9, s32[128,128]{1,0:T(8,128)} %bitcast.11, bf16[128,152,128]{2,1,0:T(8,128)(2,1)} %all_to_all.10.in_hbm), custom_call_target="tpu_custom_call" | custom-call | tf_op jit(solution)/shard_map/attend/pallas_call | solution.py:407
  103.3 47.0 %all_to_all.11 = bf16[128,88,128]{2,1,0:T(8,128)(2,1)} all-to-all(bf16[128,88,128]{2,1,0:T(8,128)(2,1)} %attend.1), channel_id=1, replica_groups=mesh['ctx'=32,'head'=4] {'ctx','head'}, dimensions={0} | all-to-all | bytes 5767168 | tf_op jit(solution)/shard_map/all_to_all | solution.py:373
  150.3 5.1 %to_rows.1 = (bf16[128,8192]{1,0:T(8,128)(2,1)}, bf16[128,1024]{1,0:T(8,128)(2,1)}, bf16[128,1024]{1,0:T(8,128)(2,1)}) custom-call(s32[1]{0:T(128)} %bitcast.me_ref, s32[128,128]{1,0:T(8,128)} %bitcast.10, bf16[16,8,88,128]{3,2,1,0:T(8,128)(2,1)} %bitcast.7), custom_call_target="tpu_custom_call" | custom-call | tf_op jit(solution)/shard_map/to_rows/pallas_call | solution.py:443

commit v4 on v3

--- a/solution.py
+++ b/solution.py
@@ -19,7 +19,7 @@
 
 SEND_ROWS = 8 * (2 * WIDTH + 3)
 BACK_ROWS = 8 * (WIDTH + 3)
-VMEM_LIMIT = 56 * 1024 * 1024
+SEND_MIB, ATTEND_MIB, RETURN_MIB = 56, 38, 20
 PER = 8
 QB = 1
 IN_ORDER = (4, 0, 1, 2, 3)
@@ -78,19 +78,23 @@
     place_copy = fetch_place(place_hbm, place_ref, me_ref[0], small.at[0])
     adv_copy = pltpu.make_async_copy(adv_hbm, adv_ref, small.at[1])
     adv_copy.start()
-    pairs = ((q_hbm, q_ref), (g_hbm, g_ref), (k_hbm, k_ref), (v_hbm, v_ref))
+    whole = [
+        pltpu.make_async_copy(k_hbm, k_ref, small.at[2]),
+        pltpu.make_async_copy(v_hbm, v_ref, small.at[3]),
+    ]
 
     def copies_in(g):
-        for i, (source, into) in enumerate(pairs):
-            width = WIDTH * D if i < 2 else D
-            at = slice(g * width, (g + 1) * width)
-            yield pltpu.make_async_copy(source.at[:, at], into.at[:, at], sems.at[i, g])
+        at = slice(g * WIDTH * D, (g + 1) * WIDTH * D)
+        return [
+            pltpu.make_async_copy(source.at[:, at], into.at[:, at], sems.at[i, g])
+            for i, (source, into) in enumerate(((q_hbm, q_ref), (g_hbm, g_ref)))
+        ]
 
     def copy_out(g):
-        return pltpu.make_async_copy(out_ref.at[:, g], out_hbm.at[:, g], sems.at[4, g])
+        return pltpu.make_async_copy(out_ref.at[:, g], out_hbm.at[:, g], sems.at[2, g])
 
     for g in range(GROUPS):
-        for copy in copies_in(g):
+        for copy in copies_in(g) + (whole if g == 0 else []):
             copy.start()
     place_copy.wait()
     adv_copy.wait()
@@ -98,7 +102,7 @@
     own, halo_k, halo_v = [onehot(rows, code) for code in token_codes(place_ref, me_ref[0])]
     weight = jnp.transpose(jnp.broadcast_to(adv_ref[...], (128, 128)))
     for g in range(GROUPS):
-        for copy in copies_in(g):
+        for copy in copies_in(g) + (whole if g == 0 else []):
             copy.wait()
         wide = slice(g * WIDTH * D, (g + 1) * WIDTH * D)
         narrow = slice(g * D, (g + 1) * D)
@@ -138,22 +142,16 @@
 
 
 def attend_kernel(
-    me_ref, place_hbm, doc_hbm, in_hbm, out_hbm,
-    place_ref, doc_ref, in_ref, out_ref, to_pos, to_src, column, arrived, qs, ws, ks, vs, kt, doc_t, dq_t, dk_acc, dv_acc, counts,
-    in_sem, out_sem, small,
+    me_ref, place_hbm, doc_hbm, in_ref, out_ref,
+    place_ref, doc_ref, to_pos, to_src, column, arrived, qs, ws, ks, vs, kt, doc_t, dq_t, dk_acc, dv_acc, counts,
+    small,
 ):
-    def copy_in(i):
-        at = pl.ds(32 * i, 32 if i < 4 else 24)
-        return pltpu.make_async_copy(in_hbm.at[:, at], in_ref.at[:, at], in_sem.at[i])
-
     tables = [
         pltpu.make_async_copy(place_hbm, place_ref, small.at[0]),
         pltpu.make_async_copy(doc_hbm, doc_ref, small.at[1]),
     ]
     for copy in tables:
         copy.start()
-    for i in IN_ORDER:
-        copy_in(i).start()
     for copy in tables:
         copy.wait()
 
@@ -198,7 +196,6 @@
         return dot(to_pos[map_at], both).astype(BF16)
 
     for i in IN_ORDER:
-        copy_in(i).wait()
         tiles = range(4 * i, min(4 * i + 4, 19))
         for t in tiles:
             arrived[t, 0], arrived[t, 1] = halves(t)
@@ -272,10 +269,6 @@
         rows = jnp.concatenate([jnp.where(upper, a, b), jnp.where(upper, b, a)], axis=1)
         return rows.reshape(1024, 128)
 
-    def copy_out(i):
-        at = pl.ds(16 * i, 16 if i < 4 else 24)
-        return pltpu.make_async_copy(out_ref.at[:, at], out_hbm.at[:, at], out_sem.at[i])
-
     def rounded(b):
         at = slice(b * BLOCK, (b + 1) * BLOCK)
         return dk_acc[at, :].astype(BF16), dv_acc[at, :].astype(BF16)
@@ -285,7 +278,6 @@
     tiles = [woven(both[0][:, i * 128 : (i + 1) * 128], both[1][:, i * 128 : (i + 1) * 128]) for i in range(2)]
     tiles.append(woven(dot(to_src[2], halo_key), dot(to_src[3], halo_value)))
     tiles_to(out_ref, 8 * WIDTH, tiles)
-    copy_out(4).start()
     for h in range(0, WIDTH, 2):
         both = [
             dot_nt(
@@ -296,25 +288,17 @@
         ]
         tiles = [woven(both[0][:, i * 128 : (i + 1) * 128], both[1][:, i * 128 : (i + 1) * 128]) for i in range(2)]
         tiles_to(out_ref, 8 * h, tiles)
-        copy_out(h // 2).start()
-    for i in range(5):
-        copy_out(i).wait()
 
 
 def return_kernel(
-    me_ref, place_hbm, in_hbm, dq_hbm, dk_hbm, dv_hbm, place_ref, in_ref, dq_ref, dk_ref, dv_ref, sems, small
+    me_ref, place_hbm, in_ref, dq_hbm, dk_hbm, dv_hbm, place_ref, dq_ref, dk_ref, dv_ref, sems, small
 ):
     place_copy = fetch_place(place_hbm, place_ref, me_ref[0], small.at[0])
 
-    def copy_in(g):
-        return pltpu.make_async_copy(in_hbm.at[:, g], in_ref.at[:, g], sems.at[0, g])
-
     def copy_dq(g):
         at = slice(g * WIDTH * D, (g + 1) * WIDTH * D)
-        return pltpu.make_async_copy(dq_ref.at[:, at], dq_hbm.at[:, at], sems.at[1, g])
-
-    for g in range(GROUPS):
-        copy_in(g).start()
+        return pltpu.make_async_copy(dq_ref.at[:, at], dq_hbm.at[:, at], sems.at[g])
+
     place_copy.wait()
 
     def column(code):
@@ -333,7 +317,6 @@
     )
     keys, values = onehot(iota((128, 128), 1), key_c), onehot(iota((128, 128), 1), value_c)
     for g in range(GROUPS):
-        copy_in(g).wait()
 
         def pair_of(tile):
             return in_ref[:, g, 8 * tile : 8 * tile + 16, :].reshape(256, 128)
@@ -363,10 +346,11 @@
 
 SMEM = pl.BlockSpec(memory_space=pltpu.SMEM)
 ANY = pl.BlockSpec(memory_space=pl.ANY)
-
-
-def params():
-    return pltpu.CompilerParams(vmem_limit_bytes=VMEM_LIMIT)
+VMEM = pl.BlockSpec(memory_space=pltpu.VMEM)
+
+
+def params(mib):
+    return pltpu.CompilerParams(vmem_limit_bytes=mib * 1024 * 1024)
 
 
 def exchanged(rows):
@@ -387,10 +371,10 @@
             pltpu.VMEM((128, GROUPS * D), BF16),
             pltpu.VMEM((128, GROUPS * D), BF16),
             pltpu.VMEM((PAIRS, GROUPS, SEND_ROWS, 128), BF16),
-            pltpu.SemaphoreType.DMA((5, GROUPS)),
-            pltpu.SemaphoreType.DMA((2,)),
+            pltpu.SemaphoreType.DMA((3, GROUPS)),
+            pltpu.SemaphoreType.DMA((4,)),
         ],
-        compiler_params=params(),
+        compiler_params=params(SEND_MIB),
         name="to_blocks",
     )(me, place2, advantage.reshape(1, 128), query, grad_out, key, value)
     return out.reshape(PAIRS * GROUPS, SEND_ROWS, 128)
@@ -406,14 +390,12 @@
     heads = pltpu.VMEM((WIDTH, 2 * BLOCK, D), BF16)
     gradients = pl.pallas_call(
         attend_kernel,
-        in_specs=[SMEM, ANY, ANY, ANY],
-        out_specs=ANY,
+        in_specs=[SMEM, ANY, ANY, VMEM],
+        out_specs=VMEM,
         out_shape=jax.ShapeDtypeStruct((128, BACK_ROWS, 128), BF16),
         scratch_shapes=[
             pltpu.VMEM((128, 128), jnp.int32),
             pltpu.VMEM((128, 128), jnp.int32),
-            pltpu.VMEM((128, SEND_ROWS, 128), BF16),
-            pltpu.VMEM((128, BACK_ROWS, 128), BF16),
             maps,
             maps,
             pltpu.VMEM((4, BLOCK, 128), F32),
@@ -428,11 +410,9 @@
             pltpu.VMEM((SPAN, D), F32),
             pltpu.VMEM((SPAN, D), F32),
             pltpu.SMEM((8,), jnp.int32),
-            pltpu.SemaphoreType.DMA((5,)),
-            pltpu.SemaphoreType.DMA((5,)),
             pltpu.SemaphoreType.DMA((2,)),
         ],
-        compiler_params=params(),
+        compiler_params=params(ATTEND_MIB),
         name="attend",
     )(me, place2, doc2, arrived)
 
@@ -442,19 +422,18 @@
     narrow = (128, GROUPS * D)
     return pl.pallas_call(
         return_kernel,
-        in_specs=[SMEM, ANY, ANY],
+        in_specs=[SMEM, ANY, VMEM],
         out_specs=[ANY] * 3,
         out_shape=[jax.ShapeDtypeStruct(x, BF16) for x in (wide, narrow, narrow)],
         scratch_shapes=[
             pltpu.VMEM((8, 128), jnp.int32),
-            pltpu.VMEM((PAIRS, GROUPS, rows, 128), BF16),
             pltpu.VMEM(wide, BF16),
             pltpu.VMEM(narrow, BF16),
             pltpu.VMEM(narrow, BF16),
-            pltpu.SemaphoreType.DMA((2, GROUPS)),
+            pltpu.SemaphoreType.DMA((GROUPS,)),
             pltpu.SemaphoreType.DMA((3,)),
         ],
-        compiler_params=params(),
+        compiler_params=params(RETURN_MIB),
         name="to_rows",
     )(me, place2, back.reshape(PAIRS, GROUPS, rows, 128))
 

time: 155 us -> 147 us (0.948)
  Pallas kernels: 34.1 us -> 27.1 us
    pallas_call x2, Pallas kernels: 28 us -> 21.1 us  [the longest x1 18.8 us: shards(): pl.pallas_call(attend_kernel, in_specs=[SMEM, ANY, ANY, VMEM], out_specs=...]
where the time goes in v4:
time: 147 us; the launch traced here: 148 us
  blocking collectives  120 us (82%)
  Pallas kernels  27.1 us (18%)
    all_to_all x2, blocking collectives, exchanged(): lax.all_to_all(rows, ('ctx', 'head'), split_axis=0, concat_axis=0, tiled=...  120 us
    pallas_call x1, Pallas kernels, shards(): pl.pallas_call(attend_kernel, in_specs=[SMEM, ANY, ANY, VMEM], out_specs=...  18.8 us
    pallas_call x1, Pallas kernels, sent(): pl.pallas_call(send_kernel, in_specs=[SMEM] + [ANY] * 6, out_specs=ANY, o...  5.96 us

profile of v4, /device:TPU:1, one launch (start us, length us, event | category | flops | bytes accessed | tf_op | source)
XLA Modules:
  0.0 147.7 jit_solution(2127228406766165219)
XLA Ops:
  0.6 6.0 %to_blocks.1 = bf16[16,8,152,128]{3,2,1,0:T(8,128)(2,1)} custom-call(s32[1]{0:T(128)} %bitcast.me_ref, s32[128,128]{1,0:T(8,128)} %bitcast.7, f32[1,128]{1,0:T(1,128)} %bitcast.12, bf16[128,8192]{1,0:T(8,128)(2,1)} %q_hbm.1, bf16[128,8192]{1,0:T(8,128)(2,1)} %g_hbm.1, bf16[128,1024]{1,0:T(8,128)(2,1)} %k_hbm.1, bf16[128,1024]{1,0:T(8,128)(2,1)} %v_hbm.1), custom_call_target="tpu_custom_call" | custom-call | tf_op jit(solution)/shard_map/to_blocks/pallas_call | solution.py:361
  6.6 0.0 copy-start
  6.6 0.0 copy-start.1
  6.6 73.5 %all_to_all.10.in_ref = bf16[128,152,128]{2,1,0:T(8,128)(2,1)S(1)} all-to-all(bf16[128,152,128]{2,1,0:T(8,128)(2,1)} %bitcast.11), channel_id=1, replica_groups=mesh['ctx'=32,'head'=4] {'ctx','head'}, dimensions={0} | all-to-all | bytes 9961472 | tf_op jit(solution)/shard_map/all_to_all | solution.py:357
  80.1 0.0 copy-done
  80.1 0.0 copy-done.1
  80.1 18.8 %attend.1 = bf16[128,88,128]{2,1,0:T(8,128)(2,1)S(1)} custom-call(s32[1]{0:T(128)} %bitcast.me_ref, s32[128,128]{1,0:T(8,128)S(1)} %bitcast.8, s32[128,128]{1,0:T(8,128)S(1)} %bitcast.10, bf16[128,152,128]{2,1,0:T(8,128)(2,1)S(1)} %all_to_all.10.in_ref), custom_call_target="tpu_custom_call" | custom-call | tf_op jit(solution)/shard_map/attend/pallas_call | solution.py:391
  98.9 46.3 %all_to_all.11 = bf16[128,88,128]{2,1,0:T(8,128)(2,1)S(1)} all-to-all(bf16[128,88,128]{2,1,0:T(8,128)(2,1)S(1)} %attend.1), channel_id=1, replica_groups=mesh['ctx'=32,'head'=4] {'ctx','head'}, dimensions={0} | all-to-all | bytes 5767168 | tf_op jit(solution)/shard_map/all_to_all | solution.py:357
  145.2 2.3 %to_rows.1 = (bf16[128,8192]{1,0:T(8,128)(2,1)}, bf16[128,1024]{1,0:T(8,128)(2,1)}, bf16[128,1024]{1,0:T(8,128)(2,1)}) custom-call(s32[1]{0:T(128)} %bitcast.me_ref, s32[128,128]{1,0:T(8,128)S(1)} %bitcast.9, bf16[16,8,88,128]{3,2,1,0:T(8,128)(2,1)S(1)} %bitcast.6), custom_call_target="tpu_custom_call" | custom-call | tf_op jit(solution)/shard_map/to_rows/pallas_call | solution.py:423
Async XLA Ops:
  6.6 73.5 %copy-start = (s32[16384]{0:T(1024)S(1)}, s32[16384]{0:T(1024)}, u32[]{:S(2)}) copy-start(s32[16384]{0:T(1024)} %param.12) | copy-start | bytes 196612
  6.6 73.5 %copy-start.1 = (s32[16384]{0:T(1024)S(1)}, s32[16384]{0:T(1024)}, u32[]{:S(2)}) copy-start(s32[16384]{0:T(1024)} %param.13) | copy-start | bytes 196612

commit v5 on v4

--- a/solution.py
+++ b/solution.py
@@ -1,3 +1,5 @@
+import functools
+
 import jax
 import jax.numpy as jnp
 from jax import lax
@@ -20,7 +22,9 @@
 SEND_ROWS = 8 * (2 * WIDTH + 3)
 BACK_ROWS = 8 * (WIDTH + 3)
 SEND_MIB, ATTEND_MIB, RETURN_MIB = 56, 38, 20
+AHEAD = 3
 PER = 8
+WINDOWS = (3, 4, 5, 6, 8, 10)
 QB = 1
 IN_ORDER = (4, 0, 1, 2, 3)
 
@@ -31,6 +35,10 @@
 
 def dot(a, b):
     return jnp.dot(a, b, preferred_element_type=F32)
+
+
+def dot_tn(a, b):
+    return lax.dot_general(a, b, (((0,), (0,)), ((), ())), preferred_element_type=F32)
 
 
 def dot_nt(a, b):
@@ -93,7 +101,7 @@
     def copy_out(g):
         return pltpu.make_async_copy(out_ref.at[:, g], out_hbm.at[:, g], sems.at[2, g])
 
-    for g in range(GROUPS):
+    for g in range(AHEAD):
         for copy in copies_in(g) + (whole if g == 0 else []):
             copy.start()
     place_copy.wait()
@@ -104,6 +112,9 @@
     for g in range(GROUPS):
         for copy in copies_in(g) + (whole if g == 0 else []):
             copy.wait()
+        if g + AHEAD < GROUPS:
+            for copy in copies_in(g + AHEAD):
+                copy.start()
         wide = slice(g * WIDTH * D, (g + 1) * WIDTH * D)
         narrow = slice(g * D, (g + 1) * D)
         grad = g_ref[:, wide]
@@ -142,19 +153,9 @@
 
 
 def attend_kernel(
-    me_ref, place_hbm, doc_hbm, in_ref, out_ref,
-    place_ref, doc_ref, to_pos, to_src, column, arrived, qs, ws, ks, vs, kt, doc_t, dq_t, dk_acc, dv_acc, counts,
-    small,
+    me_ref, place_ref, doc_ref, in_ref, out_ref,
+    to_pos, to_src, column, arrived, qs, ws, ks, vs, doc_t, dq_t, dk_acc, dv_acc, counts,
 ):
-    tables = [
-        pltpu.make_async_copy(place_hbm, place_ref, small.at[0]),
-        pltpu.make_async_copy(doc_hbm, doc_ref, small.at[1]),
-    ]
-    for copy in tables:
-        copy.start()
-    for copy in tables:
-        copy.wait()
-
     pair = lax.shift_right_logical(me_ref[0], 3)
     place = place_ref[...]
     even = (iota((128, 128), 0) & 1) == 0
@@ -167,12 +168,12 @@
 
     docs = doc_ref[...]
     block_at = iota((128, 128), 0)
-    last = iota((128, 128), 1) == 127
+    last = (iota((128, 128), 1) & 63) == 63
     for ib in range(8):
         block = 8 * pair + ib
         first_doc = doc_ref[pl.ds(block, 1), :][:, 0:1]
         near = last & (block_at < block) & (block_at >= block - 4) & (docs >= first_doc)
-        counts[ib] = 1 + jnp.sum(near.astype(F32)).astype(jnp.int32)
+        counts[ib] = 2 + jnp.sum(near.astype(F32)).astype(jnp.int32)
     for b in range(12):
         at = 8 * pair - 4 + b
         doc = doc_ref[pl.ds(jnp.maximum(at, 0), 1), :].astype(F32)
@@ -215,15 +216,14 @@
                 vs[at, :] = moved[:, 128:]
             ks[:BLOCK, :] = placed(18, 1, 0, 2)
             vs[:BLOCK, :] = placed(18, 1, 1, 3)
-            kt[...] = dot_nt(onehot(iota((128, 128), 0), iota((128, 128), 1)), ks[...]).astype(BF16)
 
     def over(first, n):
-        length = n * 128
+        length = n * 64
         for ib in [first + k for k in range(QB)]:
             rows = pl.ds(pl.multiple_of(ib * 128, 128), 128)
             query_doc = doc_ref[pl.ds(8 * pair + ib, 1), :].astype(F32)
-            window = pl.ds(pl.multiple_of((ib + 5 - n) * 128, 128), length)
-            keys, values, keys_t = ks[window, :], vs[window, :], kt[:, window]
+            window = pl.ds(pl.multiple_of((ib + 5) * 128 - length, 64), length)
+            keys, values = ks[window, :], vs[window, :]
             later = iota((length, 128), 0) - iota((length, 128), 1) > length - 128
             bias = jnp.where((doc_t[window, :] == query_doc) & ~later, 0.0, NEG)
             bias = jnp.concatenate([bias] * PER, axis=1)
@@ -238,7 +238,7 @@
                 dprob = dot_nt(values, grad)
                 delta = jnp.sum(weights.astype(F32) * dprob, axis=0, keepdims=True)
                 dscore = (prob * SCALE * (dprob - delta)).astype(BF16)
-                dq = dot(keys_t, dscore).astype(BF16)
+                dq = dot_tn(keys, dscore).astype(BF16)
                 for k in range(PER):
                     dq_t[h + k, :, rows] = dq[:, k * 128 : (k + 1) * 128]
                 all_weights.append(weights)
@@ -257,9 +257,8 @@
         count = counts[first]
         for k in range(1, QB):
             count = jnp.maximum(count, counts[first + k])
-        pl.when(count <= 2)(lambda: over(first, 2))
-        pl.when(count == 3)(lambda: over(first, 3))
-        pl.when(count >= 4)(lambda: over(first, 5))
+        for low, n in zip((0,) + WINDOWS, WINDOWS):
+            pl.when((count > low) & (count <= n))(functools.partial(over, first, n))
         return carry
 
     lax.fori_loop(0, 8 // QB, query_blocks, 0)
@@ -390,12 +389,10 @@
     heads = pltpu.VMEM((WIDTH, 2 * BLOCK, D), BF16)
     gradients = pl.pallas_call(
         attend_kernel,
-        in_specs=[SMEM, ANY, ANY, VMEM],
+        in_specs=[SMEM, VMEM, VMEM, VMEM],
         out_specs=VMEM,
         out_shape=jax.ShapeDtypeStruct((128, BACK_ROWS, 128), BF16),
         scratch_shapes=[
-            pltpu.VMEM((128, 128), jnp.int32),
-            pltpu.VMEM((128, 128), jnp.int32),
             maps,
             maps,
             pltpu.VMEM((4, BLOCK, 128), F32),
@@ -404,13 +401,11 @@
             heads,
             pltpu.VMEM((SPAN, D), BF16),
             pltpu.VMEM((SPAN, D), BF16),
-            pltpu.VMEM((D, SPAN), BF16),
             pltpu.VMEM((SPAN, 128), F32),
             pltpu.VMEM((WIDTH, D, 2 * BLOCK), BF16),
             pltpu.VMEM((SPAN, D), F32),
             pltpu.VMEM((SPAN, D), F32),
             pltpu.SMEM((8,), jnp.int32),
-            pltpu.SemaphoreType.DMA((2,)),
         ],
         compiler_params=params(ATTEND_MIB),
         name="attend",

time: 147 us -> 145 us (0.986)
  Pallas kernels: 27.1 us -> 25.3 us
    pallas_call x1, Pallas kernels: 18.8 us -> 17.2 us  [shards(): pl.pallas_call(attend_kernel, in_specs=[SMEM, VMEM, VMEM, VMEM], out_spec...]
where the time goes in v5:
time: 145 us
  blocking collectives  119 us (82%)
  Pallas kernels  25.3 us (17%)
    all_to_all x2, blocking collectives, exchanged(): lax.all_to_all(rows, ('ctx', 'head'), split_axis=0, concat_axis=0, tiled=...  119 us
    pallas_call x1, Pallas kernels, shards(): pl.pallas_call(attend_kernel, in_specs=[SMEM, VMEM, VMEM, VMEM], out_spec...  17.2 us
    pallas_call x1, Pallas kernels, sent(): pl.pallas_call(send_kernel, in_specs=[SMEM] + [ANY] * 6, out_specs=ANY, o...  5.81 us

profile of v5, /device:TPU:1, one launch (start us, length us, event | category | flops | bytes accessed | tf_op | source)
XLA Modules:
  0.0 144.7 jit_solution(580149105722151706)
XLA Ops:
  0.6 5.8 %to_blocks.1 = bf16[16,8,152,128]{3,2,1,0:T(8,128)(2,1)} custom-call(s32[1]{0:T(128)} %bitcast.me_ref, s32[128,128]{1,0:T(8,128)} %bitcast.7, f32[1,128]{1,0:T(1,128)} %bitcast.12, bf16[128,8192]{1,0:T(8,128)(2,1)} %q_hbm.1, bf16[128,8192]{1,0:T(8,128)(2,1)} %g_hbm.1, bf16[128,1024]{1,0:T(8,128)(2,1)} %k_hbm.1, bf16[128,1024]{1,0:T(8,128)(2,1)} %v_hbm.1), custom_call_target="tpu_custom_call" | custom-call | tf_op jit(solution)/shard_map/to_blocks/pallas_call | solution.py:360
  6.5 0.0 copy-start
  6.5 0.0 copy-start.1
  6.5 73.5 %all_to_all.10.in_ref = bf16[128,152,128]{2,1,0:T(8,128)(2,1)S(1)} all-to-all(bf16[128,152,128]{2,1,0:T(8,128)(2,1)} %bitcast.11), channel_id=1, replica_groups=mesh['ctx'=32,'head'=4] {'ctx','head'}, dimensions={0} | all-to-all | bytes 9961472 | tf_op jit(solution)/shard_map/all_to_all | solution.py:356
  80.0 0.0 copy-done
  80.0 0.0 copy-done.1
  80.0 17.2 %attend.1 = bf16[128,88,128]{2,1,0:T(8,128)(2,1)S(1)} custom-call(s32[1]{0:T(128)} %bitcast.me_ref, s32[128,128]{1,0:T(8,128)S(1)} %bitcast.8, s32[128,128]{1,0:T(8,128)S(1)} %bitcast.10, bf16[128,152,128]{2,1,0:T(8,128)(2,1)S(1)} %all_to_all.10.in_ref), custom_call_target="tpu_custom_call" | custom-call | tf_op jit(solution)/shard_map/attend/pallas_call | solution.py:390
  97.2 45.0 %all_to_all.11 = bf16[128,88,128]{2,1,0:T(8,128)(2,1)S(1)} all-to-all(bf16[128,88,128]{2,1,0:T(8,128)(2,1)S(1)} %attend.1), channel_id=1, replica_groups=mesh['ctx'=32,'head'=4] {'ctx','head'}, dimensions={0} | all-to-all | bytes 5767168 | tf_op jit(solution)/shard_map/all_to_all | solution.py:356
  142.2 2.3 %to_rows.1 = (bf16[128,8192]{1,0:T(8,128)(2,1)}, bf16[128,1024]{1,0:T(8,128)(2,1)}, bf16[128,1024]{1,0:T(8,128)(2,1)}) custom-call(s32[1]{0:T(128)} %bitcast.me_ref, s32[128,128]{1,0:T(8,128)S(1)} %bitcast.9, bf16[16,8,88,128]{3,2,1,0:T(8,128)(2,1)S(1)} %bitcast.6), custom_call_target="tpu_custom_call" | custom-call | tf_op jit(solution)/shard_map/to_rows/pallas_call | solution.py:418
Async XLA Ops:
  6.5 73.5 %copy-start = (s32[16384]{0:T(1024)S(1)}, s32[16384]{0:T(1024)}, u32[]{:S(2)}) copy-start(s32[16384]{0:T(1024)} %param.12) | copy-start | bytes 196612
  6.5 73.5 %copy-start.1 = (s32[16384]{0:T(1024)S(1)}, s32[16384]{0:T(1024)}, u32[]{:S(2)}) copy-start(s32[16384]{0:T(1024)} %param.13) | copy-start | bytes 196612

commit v6 on v5

--- a/solution.py
+++ b/solution.py
@@ -227,27 +227,23 @@
             later = iota((length, 128), 0) - iota((length, 128), 1) > length - 128
             bias = jnp.where((doc_t[window, :] == query_doc) & ~later, 0.0, NEG)
             bias = jnp.concatenate([bias] * PER, axis=1)
-            all_weights, all_dscore, all_query, all_grad = [], [], [], []
+            all_dscore, all_query = [], []
             for h in range(0, WIDTH, PER):
                 query = jnp.concatenate([qs[h + k, rows, :] for k in range(PER)], axis=0)
                 grad = jnp.concatenate([ws[h + k, rows, :] for k in range(PER)], axis=0)
                 score = dot_nt(keys, query) * (SCALE * LOG2E) + bias
+                dprob = dot_nt(values, grad)
                 prob = jnp.exp2(score - jnp.max(score, axis=0, keepdims=True))
                 prob = prob * (1.0 / jnp.sum(prob, axis=0, keepdims=True))
                 weights = prob.astype(BF16)
-                dprob = dot_nt(values, grad)
+                dv_acc[window, :] += dot(weights, grad)
                 delta = jnp.sum(weights.astype(F32) * dprob, axis=0, keepdims=True)
                 dscore = (prob * SCALE * (dprob - delta)).astype(BF16)
                 dq = dot_tn(keys, dscore).astype(BF16)
                 for k in range(PER):
                     dq_t[h + k, :, rows] = dq[:, k * 128 : (k + 1) * 128]
-                all_weights.append(weights)
                 all_dscore.append(dscore)
                 all_query.append(query)
-                all_grad.append(grad)
-            dv_acc[window, :] += dot(
-                jnp.concatenate(all_weights, axis=1), jnp.concatenate(all_grad, axis=0)
-            )
             dk_acc[window, :] += dot(
                 jnp.concatenate(all_dscore, axis=1), jnp.concatenate(all_query, axis=0)
             )

time: 145 us -> 145 us (level)
  Pallas kernels: 25.3 us -> 23.4 us
    pallas_call x1, Pallas kernels: 17.2 us -> 15.3 us  [shards(): pl.pallas_call(attend_kernel, in_specs=[SMEM, VMEM, VMEM, VMEM], out_spec...]
where the time goes in v6:
time: 145 us; the launch traced here: 144 us
  blocking collectives  120 us (83%)
  Pallas kernels  23.4 us (16%)
    all_to_all x2, blocking collectives, exchanged(): lax.all_to_all(rows, ('ctx', 'head'), split_axis=0, concat_axis=0, tiled=...  120 us
    pallas_call x1, Pallas kernels, shards(): pl.pallas_call(attend_kernel, in_specs=[SMEM, VMEM, VMEM, VMEM], out_spec...  15.3 us
    pallas_call x1, Pallas kernels, sent(): pl.pallas_call(send_kernel, in_specs=[SMEM] + [ANY] * 6, out_specs=ANY, o...  5.81 us

profile of v6, /device:TPU:1, one launch (start us, length us, event | category | flops | bytes accessed | tf_op | source)
XLA Modules:
  0.0 144.1 jit_solution(7763623888882150093)
XLA Ops:
  0.6 5.8 %to_blocks.1 = bf16[16,8,152,128]{3,2,1,0:T(8,128)(2,1)} custom-call(s32[1]{0:T(128)} %bitcast.me_ref, s32[128,128]{1,0:T(8,128)} %bitcast.7, f32[1,128]{1,0:T(1,128)} %bitcast.12, bf16[128,8192]{1,0:T(8,128)(2,1)} %q_hbm.1, bf16[128,8192]{1,0:T(8,128)(2,1)} %g_hbm.1, bf16[128,1024]{1,0:T(8,128)(2,1)} %k_hbm.1, bf16[128,1024]{1,0:T(8,128)(2,1)} %v_hbm.1), custom_call_target="tpu_custom_call" | custom-call | tf_op jit(solution)/shard_map/to_blocks/pallas_call | solution.py:356
  6.5 0.0 copy-start
  6.5 0.0 copy-start.1
  6.5 73.5 %all_to_all.10.in_ref = bf16[128,152,128]{2,1,0:T(8,128)(2,1)S(1)} all-to-all(bf16[128,152,128]{2,1,0:T(8,128)(2,1)} %bitcast.11), channel_id=1, replica_groups=mesh['ctx'=32,'head'=4] {'ctx','head'}, dimensions={0} | all-to-all | bytes 9961472 | tf_op jit(solution)/shard_map/all_to_all | solution.py:352
  80.0 0.0 copy-done
  80.0 0.0 copy-done.1
  80.0 15.3 %attend.1 = bf16[128,88,128]{2,1,0:T(8,128)(2,1)S(1)} custom-call(s32[1]{0:T(128)} %bitcast.me_ref, s32[128,128]{1,0:T(8,128)S(1)} %bitcast.8, s32[128,128]{1,0:T(8,128)S(1)} %bitcast.10, bf16[128,152,128]{2,1,0:T(8,128)(2,1)S(1)} %all_to_all.10.in_ref), custom_call_target="tpu_custom_call" | custom-call | tf_op jit(solution)/shard_map/attend/pallas_call | solution.py:386
  95.3 46.3 %all_to_all.11 = bf16[128,88,128]{2,1,0:T(8,128)(2,1)S(1)} all-to-all(bf16[128,88,128]{2,1,0:T(8,128)(2,1)S(1)} %attend.1), channel_id=1, replica_groups=mesh['ctx'=32,'head'=4] {'ctx','head'}, dimensions={0} | all-to-all | bytes 5767168 | tf_op jit(solution)/shard_map/all_to_all | solution.py:352
  141.6 2.3 %to_rows.1 = (bf16[128,8192]{1,0:T(8,128)(2,1)}, bf16[128,1024]{1,0:T(8,128)(2,1)}, bf16[128,1024]{1,0:T(8,128)(2,1)}) custom-call(s32[1]{0:T(128)} %bitcast.me_ref, s32[128,128]{1,0:T(8,128)S(1)} %bitcast.9, bf16[16,8,88,128]{3,2,1,0:T(8,128)(2,1)S(1)} %bitcast.6), custom_call_target="tpu_custom_call" | custom-call | tf_op jit(solution)/shard_map/to_rows/pallas_call | solution.py:414
Async XLA Ops:
  6.5 73.5 %copy-start = (s32[16384]{0:T(1024)S(1)}, s32[16384]{0:T(1024)}, u32[]{:S(2)}) copy-start(s32[16384]{0:T(1024)} %param.12) | copy-start | bytes 196612
  6.5 73.5 %copy-start.1 = (s32[16384]{0:T(1024)S(1)}, s32[16384]{0:T(1024)}, u32[]{:S(2)}) copy-start(s32[16384]{0:T(1024)} %param.13) | copy-start | bytes 196612
